TPU v7x, 512 devices: a whole 4x4x16 slice. The times are simulated.
512 devices in a mesh: range: 32 (over x, z_lo), height: 16 (over y, z_hi, core).
Axes of the slice: x: 4, y: 4, z: 16 (z_hi: 2, z_lo: 8; z = z_hi * 8 + z_lo), core: 2. Of those that a mesh axis runs over, the one named last changes fastest.
Arguments:
- pressure: float32 [1536, 128, 128], P('range', 'height'), may hold values from -6 to 6
- vertical_flow: float32 [1536, 128, 128], P('range', 'height'), may hold values from -6 to 6
- radial_flow: float32 [1536, 128, 128], P('range', 'height'), may hold values from -6 to 6
- lateral_flow: float32 [1536, 128, 128], P('range', 'height'), may hold values from -6 to 6
- stiffness: float32 [128, 128], P('height'), may hold values from 0.3 to 0.8
- buoyancy: float32 [128, 128], P('height'), may hold values from 0.12 to 0.25
- wind_profile: float32 [128], replicated, may hold values from -0.15 to 0.15
Outputs:
- final_pressure: float32 [1536, 128, 128], P('range', 'height')
- final_vertical: float32 [1536, 128, 128], P('range', 'height')
- final_radial: float32 [1536, 128, 128], P('range', 'height')
- final_lateral: float32 [1536, 128, 128], P('range', 'height')
All inputs are finite; a program needn't handle non-finite values.
Results may differ from a plain program's by a relative error of at most 0.00002.
Values sent between devices are 32-bit elements; how exact they have to be, the bound alone decides.
A program may use at most 64 MiB of HBM per device.

v0:
```python
import jax
import jax.numpy as jnp
from jax import lax
from jax.sharding import PartitionSpec as P

SHIFT = 8
STEPS = 2


def extended(block, sides, width):
    for axis, dim in sides:
        count = lax.axis_size(axis)
        forward = [(i, i + 1) for i in range(count - 1)]
        backward = [(target, source) for source, target in forward]
        low = lax.ppermute(
            lax.slice_in_dim(block, block.shape[dim] - width, None, axis=dim), axis, forward
        )
        high = lax.ppermute(lax.slice_in_dim(block, 0, width, axis=dim), axis, backward)
        block = jnp.concatenate([low, block, high], axis=dim)
    return block


def shifted(value, axis, steps):
    count = lax.axis_size(axis)
    first, last = (max(0, -steps), min(count, count - steps))
    return lax.ppermute(value, axis, [(source, source + steps) for source in range(first, last)])


def piece(padded, start, count, axis):
    return lax.slice_in_dim(padded, start, start + count, axis=axis)


def forward_diff(padded, axis, base, count):
    return (
        27.0 * (piece(padded, base + 1, count, axis) - piece(padded, base, count, axis))
        - (piece(padded, base + 2, count, axis) - piece(padded, base - 1, count, axis))
    ) / 24.0


def backward_diff(padded, axis, base, count):
    return (
        27.0 * (piece(padded, base, count, axis) - piece(padded, base - 1, count, axis))
        - (piece(padded, base + 1, count, axis) - piece(padded, base - 2, count, axis))
    ) / 24.0


def central_diff(padded, axis, base, count):
    return (
        8.0 * (piece(padded, base + 1, count, axis) - piece(padded, base - 1, count, axis))
        - (piece(padded, base + 2, count, axis) - piece(padded, base - 2, count, axis))
    ) / 12.0


def lateral_forward(field):
    return (
        27.0 * (jnp.roll(field, -1, -1) - field)
        - (jnp.roll(field, -2, -1) - jnp.roll(field, 1, -1))
    ) / 24.0


def lateral_backward(field):
    return (
        27.0 * (field - jnp.roll(field, 1, -1)) - (jnp.roll(field, -1, -1) - jnp.roll(field, 2, -1))
    ) / 24.0


def height_pad(pair):
    return extended(pair, (("height", 2),), 2)


def first_round(state):
    ranged = extended(state, (("range", 1),), 2)
    return (ranged, height_pad(state[:2]))


def second_round(radial_new, vert_new):
    radial_pad = extended(radial_new, (("range", 0),), 2)
    vert_pad = extended(vert_new, (("height", 1),), 2)
    return (radial_pad, vert_pad)


def advance(state, stiff, buoy, advect, shear):
    count_r = state.shape[1]
    count_h = state.shape[2]
    ranged, heights = first_round(state)
    press, vert, radial, lateral = (state[0], state[1], state[2], state[3])
    vert_h = heights[1]
    radial_new = (
        radial
        - buoy * forward_diff(ranged[0], 0, 2, count_r)
        - advect * central_diff(ranged[2], 0, 2, count_r)
        - shear * 0.5 * (piece(vert_h, 2, count_h, 1) + piece(vert_h, 1, count_h, 1))
    )
    lateral_new = (
        lateral - buoy * lateral_forward(press) - advect * central_diff(ranged[3], 0, 2, count_r)
    )
    vert_new = (
        vert
        - buoy * forward_diff(heights[0], 1, 2, count_h)
        - advect * central_diff(ranged[1], 0, 2, count_r)
    )
    radial_pad, vert_pad = second_round(radial_new, vert_new)
    spread = (
        backward_diff(radial_pad, 0, 2, count_r)
        + lateral_backward(lateral_new)
        + backward_diff(vert_pad, 1, 2, count_h)
    )
    press_new = press - stiff * spread - advect * central_diff(ranged[0], 0, 2, count_r)
    return jnp.stack((press_new, vert_new, radial_new, lateral_new))


def on_device(
    pressure, vertical_flow, radial_flow, lateral_flow, stiffness, buoyancy, wind_profile
):
    count_h = pressure.shape[1]
    edged = jnp.concatenate([wind_profile[:1], wind_profile, wind_profile[-1:]])
    shear_whole = 0.5 * (edged[2:] - edged[:-2])
    offset = lax.axis_index("height") * count_h
    advect = lax.dynamic_slice_in_dim(wind_profile, offset, count_h)[None, :, None]
    shear = lax.dynamic_slice_in_dim(shear_whole, offset, count_h)[None, :, None]
    stiff = stiffness[None]
    buoy = buoyancy[None]
    state = jnp.stack((pressure, vertical_flow, radial_flow, lateral_flow))
    for step in range(STEPS):
        state = advance(state, stiff, buoy, advect, shear)
        if step + 1 == STEPS // 2:
            arriving = shifted(state[:, :SHIFT], "range", -1)
            state = jnp.concatenate([state[:, SHIFT:], arriving], axis=1)
    return (state[0], state[1], state[2], state[3])


def solution(mesh):
    in_specs = (
        P("range", "height", None),
        P("range", "height", None),
        P("range", "height", None),
        P("range", "height", None),
        P("height", None),
        P("height", None),
        P(),
    )
    out_specs = (
        P("range", "height", None),
        P("range", "height", None),
        P("range", "height", None),
        P("range", "height", None),
    )
    return jax.shard_map(
        on_device, mesh=mesh, in_specs=in_specs, out_specs=out_specs, check_vma=False
    )
```

profile of v0, /device:TPU:10, one launch (start us, length us, event | category | flops | bytes accessed | tf_op | source)
XLA Modules:
  0.0 158.7 jit_solution(10822280798607432532)
XLA Ops:
  0.7 0.9 pad_maximum_fusion.22
  1.5 13.1 %collective-permute-start = (f32[4,2,8,128]{3,2,1,0:T(8,128)S(1)}, f32[4,2,8,128]{3,2,1,0:T(8,128)S(1)}, u32[]{:S(2)}, u32[]{:S(2)}) collective-permute-start(f32[4,2,8,128]{3,2,1,0:T(8,128)S(1)} %get-tuple-element.16), channel_id=1, source_target_pairs={{16,0},{32,16},{48,32},{64,48},{80,64},{96,80},{112,96},{128,112},... | collective-permute-start | bytes 98312 | tf_op jit(solution)/shard_map/ppermute | solution.py:18
  14.6 1.9 %collective-permute-start.1 = (f32[4,2,8,128]{3,2,1,0:T(8,128)S(1)}, f32[4,2,8,128]{3,2,1,0:T(8,128)S(1)}, u32[]{:S(2)}, u32[]{:S(2)}) collective-permute-start(f32[4,2,8,128]{3,2,1,0:T(8,128)S(1)} %get-tuple-element.17), channel_id=1, source_target_pairs={{0,16},{16,32},{32,48},{48,64},{64,80},{80,96},{96,112},{112,128},... | collective-permute-start | bytes 98312 | tf_op jit(solution)/shard_map/ppermute | solution.py:15
  16.7 1.9 %collective-permute-start.2 = (f32[2,48,2,128]{3,2,1,0:T(2,128)S(1)}, f32[2,48,2,128]{3,2,1,0:T(2,128)S(1)}, u32[]{:S(2)}, u32[]{:S(2)}) collective-permute-start(f32[2,48,2,128]{3,2,1,0:T(2,128)S(1)} %get-tuple-element.18), channel_id=1, source_target_pairs={{0,1},{1,2},{2,3},{3,4},{4,5},{5,6},{6,7},{7,8},{8,9},{9,10},{10,1... | collective-permute-start | bytes 294920 | tf_op jit(solution)/shard_map/ppermute | solution.py:15
  18.6 13.3 %collective-permute-start.3 = (f32[2,48,2,128]{3,2,1,0:T(2,128)S(1)}, f32[2,48,2,128]{3,2,1,0:T(2,128)S(1)}, u32[]{:S(2)}, u32[]{:S(2)}) collective-permute-start(f32[2,48,2,128]{3,2,1,0:T(2,128)S(1)} %get-tuple-element.19), channel_id=1, source_target_pairs={{1,0},{2,1},{3,2},{4,3},{5,4},{6,5},{7,6},{8,7},{9,8},{10,9},{11,1... | collective-permute-start | bytes 294920 | tf_op jit(solution)/shard_map/ppermute | solution.py:18
  31.9 0.1 fusion.113
  32.0 0.1 fusion.114
  32.1 0.6 copy-done.7
  32.8 0.6 fusion.115
  33.4 0.7 copy-done.9
  34.1 1.4 pad_maximum_fusion.23
  35.8 0.8 copy-done.3
  36.8 0.2 fusion.79
  37.0 0.1 fusion.110
  37.1 0.1 pad_maximum_fusion.3
  37.4 0.2 fusion.70
  37.5 0.2 fusion.83
  37.7 11.4 %collective-permute-start.5 = (f32[2,8,128]{2,1,0:T(8,128)S(1)}, f32[2,8,128]{2,1,0:T(8,128)S(1)}, u32[]{:S(2)}, u32[]{:S(2)}) collective-permute-start(f32[2,8,128]{2,1,0:T(8,128)S(1)} %get-tuple-element.36), channel_id=1, source_target_pairs={{16,0},{32,16},{48,32},{64,48},{80,64},{96,80},{112,96},{128,112},... | collective-permute-start | bytes 24584 | tf_op jit(solution)/shard_map/ppermute | solution.py:18
  49.1 1.9 %collective-permute-start.4 = (f32[2,8,128]{2,1,0:T(8,128)S(1)}, f32[2,8,128]{2,1,0:T(8,128)S(1)}, u32[]{:S(2)}, u32[]{:S(2)}) collective-permute-start(f32[2,8,128]{2,1,0:T(8,128)S(1)} %get-tuple-element.37), channel_id=1, source_target_pairs={{0,16},{16,32},{32,48},{48,64},{64,80},{80,96},{96,112},{112,128},... | collective-permute-start | bytes 24584 | tf_op jit(solution)/shard_map/ppermute | solution.py:15
  51.1 10.1 %collective-permute-start.7 = (f32[48,2,128]{2,1,0:T(2,128)S(1)}, f32[48,2,128]{2,1,0:T(2,128)S(1)}, u32[]{:S(2)}, u32[]{:S(2)}) collective-permute-start(f32[48,2,128]{2,1,0:T(2,128)S(1)} %get-tuple-element.38), channel_id=1, source_target_pairs={{1,0},{2,1},{3,2},{4,3},{5,4},{6,5},{7,6},{8,7},{9,8},{10,9},{11,1... | collective-permute-start | bytes 147464 | tf_op jit(solution)/shard_map/ppermute | solution.py:18
  61.2 1.9 %collective-permute-start.6 = (f32[48,2,128]{2,1,0:T(2,128)S(1)}, f32[48,2,128]{2,1,0:T(2,128)S(1)}, u32[]{:S(2)}, u32[]{:S(2)}) collective-permute-start(f32[48,2,128]{2,1,0:T(2,128)S(1)} %get-tuple-element.39), channel_id=1, source_target_pairs={{0,1},{1,2},{2,3},{3,4},{4,5},{5,6},{6,7},{7,8},{8,9},{9,10},{10,1... | collective-permute-start | bytes 147464 | tf_op jit(solution)/shard_map/ppermute | solution.py:15
  63.1 0.1 fusion.109
  63.2 0.1 slice.638
  63.4 12.8 %collective-permute-done.6 = f32[48,2,128]{2,1,0:T(2,128)S(1)} collective-permute-done((f32[48,2,128]{2,1,0:T(2,128)S(1)}, f32[48,2,128]{2,1,0:T(2,128)S(1)}, u32[]{:S(2)}, u32[]{:S(2)}) %collective-permute-start.6) | collective-permute-done | bytes 49184 | tf_op jit(solution)/shard_map/ppermute | solution.py:15
  76.2 0.3 fusion.19
  76.6 11.3 %collective-permute-start.9 = (f32[4,2,8,128]{3,2,1,0:T(8,128)S(1)}, f32[4,2,8,128]{3,2,1,0:T(8,128)S(1)}, u32[]{:S(2)}, u32[]{:S(2)}) collective-permute-start(f32[4,2,8,128]{3,2,1,0:T(8,128)S(1)} %pad_maximum_fusion.18), channel_id=1, source_target_pairs={{16,0},{32,16},{48,32},{64,48},{80,64},{96,80},{112,96},{128,112},... | collective-permute-start | bytes 98312 | tf_op jit(solution)/shard_map/ppermute | solution.py:18
  87.8 1.9 %collective-permute-start.8 = (f32[4,8,8,128]{3,2,1,0:T(8,128)S(1)}, f32[4,8,8,128]{3,2,1,0:T(8,128)S(1)}, u32[]{:S(2)}, u32[]{:S(2)}) collective-permute-start(f32[4,8,8,128]{3,2,1,0:T(8,128)S(1)} %pad_maximum_fusion.15), channel_id=1, source_target_pairs={{16,0},{32,16},{48,32},{64,48},{80,64},{96,80},{112,96},{128,112},... | collective-permute-start | bytes 393224 | tf_op jit(solution)/shard_map/ppermute | solution.py:26
  89.9 5.9 %collective-permute-done.8 = f32[4,8,8,128]{3,2,1,0:T(8,128)S(1)} collective-permute-done((f32[4,8,8,128]{3,2,1,0:T(8,128)S(1)}, f32[4,8,8,128]{3,2,1,0:T(8,128)S(1)}, u32[]{:S(2)}, u32[]{:S(2)}) %collective-permute-start.8) | collective-permute-done | bytes 131104 | tf_op jit(solution)/shard_map/ppermute | solution.py:26
  95.8 1.9 %collective-permute-start.10 = (f32[4,2,8,128]{3,2,1,0:T(8,128)S(1)}, f32[4,2,8,128]{3,2,1,0:T(8,128)S(1)}, u32[]{:S(2)}, u32[]{:S(2)}) collective-permute-start(f32[4,2,8,128]{3,2,1,0:T(8,128)S(1)} %slice.661), channel_id=1, source_target_pairs={{0,16},{16,32},{32,48},{48,64},{64,80},{80,96},{96,112},{112,128},... | collective-permute-start | bytes 98312 | tf_op jit(solution)/shard_map/ppermute | solution.py:15
  97.7 1.9 %collective-permute-start.11 = (f32[2,48,2,128]{3,2,1,0:T(2,128)S(1)}, f32[2,48,2,128]{3,2,1,0:T(2,128)S(1)}, u32[]{:S(2)}, u32[]{:S(2)}) collective-permute-start(f32[2,48,2,128]{3,2,1,0:T(2,128)S(1)} %get-tuple-element.10), channel_id=1, source_target_pairs={{0,1},{1,2},{2,3},{3,4},{4,5},{5,6},{6,7},{7,8},{8,9},{9,10},{10,1... | collective-permute-start | bytes 294920 | tf_op jit(solution)/shard_map/ppermute | solution.py:15
  99.7 13.3 %collective-permute-start.12 = (f32[2,48,2,128]{3,2,1,0:T(2,128)S(1)}, f32[2,48,2,128]{3,2,1,0:T(2,128)S(1)}, u32[]{:S(2)}, u32[]{:S(2)}) collective-permute-start(f32[2,48,2,128]{3,2,1,0:T(2,128)S(1)} %get-tuple-element.11), channel_id=1, source_target_pairs={{1,0},{2,1},{3,2},{4,3},{5,4},{6,5},{7,6},{8,7},{9,8},{10,9},{11,1... | collective-permute-start | bytes 294920 | tf_op jit(solution)/shard_map/ppermute | solution.py:18
  113.0 0.1 pad_maximum_fusion.1
  113.1 0.3 collective-permute-done.11
  113.4 1.7 %collective-permute-done.12 = f32[2,48,2,128]{3,2,1,0:T(2,128)S(1)} collective-permute-done((f32[2,48,2,128]{3,2,1,0:T(2,128)S(1)}, f32[2,48,2,128]{3,2,1,0:T(2,128)S(1)}, u32[]{:S(2)}, u32[]{:S(2)}) %collective-permute-start.12) | collective-permute-done | bytes 98336 | tf_op jit(solution)/shard_map/ppermute | solution.py:18
  115.1 0.2 pad_maximum_fusion.5
  115.3 0.2 fusion.38
  115.6 0.1 fusion.106
  115.7 0.1 fusion.105
  115.9 11.4 %collective-permute-start.14 = (f32[2,8,128]{2,1,0:T(8,128)S(1)}, f32[2,8,128]{2,1,0:T(8,128)S(1)}, u32[]{:S(2)}, u32[]{:S(2)}) collective-permute-start(f32[2,8,128]{2,1,0:T(8,128)S(1)} %get-tuple-element.28), channel_id=1, source_target_pairs={{16,0},{32,16},{48,32},{64,48},{80,64},{96,80},{112,96},{128,112},... | collective-permute-start | bytes 24584 | tf_op jit(solution)/shard_map/ppermute | solution.py:18
  127.3 1.9 %collective-permute-start.13 = (f32[2,8,128]{2,1,0:T(8,128)S(1)}, f32[2,8,128]{2,1,0:T(8,128)S(1)}, u32[]{:S(2)}, u32[]{:S(2)}) collective-permute-start(f32[2,8,128]{2,1,0:T(8,128)S(1)} %get-tuple-element.29), channel_id=1, source_target_pairs={{0,16},{16,32},{32,48},{48,64},{64,80},{80,96},{96,112},{112,128},... | collective-permute-start | bytes 24584 | tf_op jit(solution)/shard_map/ppermute | solution.py:15
  129.2 0.1 fusion.46
  129.4 13.1 %collective-permute-start.16 = (f32[48,2,128]{2,1,0:T(2,128)S(1)}, f32[48,2,128]{2,1,0:T(2,128)S(1)}, u32[]{:S(2)}, u32[]{:S(2)}) collective-permute-start(f32[48,2,128]{2,1,0:T(2,128)S(1)} %get-tuple-element.30), channel_id=1, source_target_pairs={{1,0},{2,1},{3,2},{4,3},{5,4},{6,5},{7,6},{8,7},{9,8},{10,9},{11,1... | collective-permute-start | bytes 147464 | tf_op jit(solution)/shard_map/ppermute | solution.py:18
  142.6 1.9 %collective-permute-start.15 = (f32[48,2,128]{2,1,0:T(2,128)S(1)}, f32[48,2,128]{2,1,0:T(2,128)S(1)}, u32[]{:S(2)}, u32[]{:S(2)}) collective-permute-start(f32[48,2,128]{2,1,0:T(2,128)S(1)} %get-tuple-element.31), channel_id=1, source_target_pairs={{0,1},{1,2},{2,3},{3,4},{4,5},{5,6},{6,7},{7,8},{8,9},{9,10},{10,1... | collective-permute-start | bytes 147464 | tf_op jit(solution)/shard_map/ppermute | solution.py:15
  144.5 0.3 fusion.31
  144.9 0.1 fusion.103
  145.0 0.1 slice.696
  145.2 12.4 %collective-permute-done.15 = f32[48,2,128]{2,1,0:T(2,128)S(1)} collective-permute-done((f32[48,2,128]{2,1,0:T(2,128)S(1)}, f32[48,2,128]{2,1,0:T(2,128)S(1)}, u32[]{:S(2)}, u32[]{:S(2)}) %collective-permute-start.15) | collective-permute-done | bytes 49184 | tf_op jit(solution)/shard_map/ppermute | solution.py:15
  157.6 1.0 fusion.9
  (52 shorter events, 1.3 us)
Async XLA Ops:
  0.6 15.9 %copy-start = (f32[48,8,128]{2,1,0:T(8,128)S(1)}, f32[48,8,128]{2,1,0:T(8,128)}, u32[]{:S(2)}) copy-start(f32[48,8,128]{2,1,0:T(8,128)} %param.7) | copy-start | bytes 589828
  0.6 15.9 %copy-start.2 = (f32[48,8,128]{2,1,0:T(8,128)S(1)}, f32[48,8,128]{2,1,0:T(8,128)}, u32[]{:S(2)}) copy-start(f32[48,8,128]{2,1,0:T(8,128)} %param.8) | copy-start | bytes 589828
  1.5 34.2 %collective-permute-start = (f32[4,2,8,128]{3,2,1,0:T(8,128)S(1)}, f32[4,2,8,128]{3,2,1,0:T(8,128)S(1)}, u32[]{:S(2)}, u32[]{:S(2)}) collective-permute-start(f32[4,2,8,128]{3,2,1,0:T(8,128)S(1)} %get-tuple-element.16), channel_id=1, source_target_pairs={{16,0},{32,16},{48,32},{64,48},{80,64},{96,80},{112,96},{128,112},... | collective-permute-start | bytes 98312 | tf_op jit(solution)/shard_map/ppermute | solution.py:18
  14.6 21.1 %collective-permute-start.1 = (f32[4,2,8,128]{3,2,1,0:T(8,128)S(1)}, f32[4,2,8,128]{3,2,1,0:T(8,128)S(1)}, u32[]{:S(2)}, u32[]{:S(2)}) collective-permute-start(f32[4,2,8,128]{3,2,1,0:T(8,128)S(1)} %get-tuple-element.17), channel_id=1, source_target_pairs={{0,16},{16,32},{32,48},{48,64},{64,80},{80,96},{96,112},{112,128},... | collective-permute-start | bytes 98312 | tf_op jit(solution)/shard_map/ppermute | solution.py:15
  16.7 20.5 %collective-permute-start.2 = (f32[2,48,2,128]{3,2,1,0:T(2,128)S(1)}, f32[2,48,2,128]{3,2,1,0:T(2,128)S(1)}, u32[]{:S(2)}, u32[]{:S(2)}) collective-permute-start(f32[2,48,2,128]{3,2,1,0:T(2,128)S(1)} %get-tuple-element.18), channel_id=1, source_target_pairs={{0,1},{1,2},{2,3},{3,4},{4,5},{5,6},{6,7},{7,8},{8,9},{9,10},{10,1... | collective-permute-start | bytes 294920 | tf_op jit(solution)/shard_map/ppermute | solution.py:15
  18.6 18.6 %collective-permute-start.3 = (f32[2,48,2,128]{3,2,1,0:T(2,128)S(1)}, f32[2,48,2,128]{3,2,1,0:T(2,128)S(1)}, u32[]{:S(2)}, u32[]{:S(2)}) collective-permute-start(f32[2,48,2,128]{3,2,1,0:T(2,128)S(1)} %get-tuple-element.19), channel_id=1, source_target_pairs={{1,0},{2,1},{3,2},{4,3},{5,4},{6,5},{7,6},{8,7},{9,8},{10,9},{11,1... | collective-permute-start | bytes 294920 | tf_op jit(solution)/shard_map/ppermute | solution.py:18
  32.1 0.7 copy-start.7
  32.1 1.3 copy-start.8
  33.4 0.7 copy-start.9
  35.6 0.9 copy-start.3
  35.6 1.0 copy-start.4
  37.7 25.7 %collective-permute-start.5 = (f32[2,8,128]{2,1,0:T(8,128)S(1)}, f32[2,8,128]{2,1,0:T(8,128)S(1)}, u32[]{:S(2)}, u32[]{:S(2)}) collective-permute-start(f32[2,8,128]{2,1,0:T(8,128)S(1)} %get-tuple-element.36), channel_id=1, source_target_pairs={{16,0},{32,16},{48,32},{64,48},{80,64},{96,80},{112,96},{128,112},... | collective-permute-start | bytes 24584 | tf_op jit(solution)/shard_map/ppermute | solution.py:18
  49.1 14.2 %collective-permute-start.4 = (f32[2,8,128]{2,1,0:T(8,128)S(1)}, f32[2,8,128]{2,1,0:T(8,128)S(1)}, u32[]{:S(2)}, u32[]{:S(2)}) collective-permute-start(f32[2,8,128]{2,1,0:T(8,128)S(1)} %get-tuple-element.37), channel_id=1, source_target_pairs={{0,16},{16,32},{32,48},{48,64},{64,80},{80,96},{96,112},{112,128},... | collective-permute-start | bytes 24584 | tf_op jit(solution)/shard_map/ppermute | solution.py:15
  51.1 12.3 %collective-permute-start.7 = (f32[48,2,128]{2,1,0:T(2,128)S(1)}, f32[48,2,128]{2,1,0:T(2,128)S(1)}, u32[]{:S(2)}, u32[]{:S(2)}) collective-permute-start(f32[48,2,128]{2,1,0:T(2,128)S(1)} %get-tuple-element.38), channel_id=1, source_target_pairs={{1,0},{2,1},{3,2},{4,3},{5,4},{6,5},{7,6},{8,7},{9,8},{10,9},{11,1... | collective-permute-start | bytes 147464 | tf_op jit(solution)/shard_map/ppermute | solution.py:18
  61.2 15.0 %collective-permute-start.6 = (f32[48,2,128]{2,1,0:T(2,128)S(1)}, f32[48,2,128]{2,1,0:T(2,128)S(1)}, u32[]{:S(2)}, u32[]{:S(2)}) collective-permute-start(f32[48,2,128]{2,1,0:T(2,128)S(1)} %get-tuple-element.39), channel_id=1, source_target_pairs={{0,1},{1,2},{2,3},{3,4},{4,5},{5,6},{6,7},{7,8},{8,9},{9,10},{10,1... | collective-permute-start | bytes 147464 | tf_op jit(solution)/shard_map/ppermute | solution.py:15
  76.6 36.4 %collective-permute-start.9 = (f32[4,2,8,128]{3,2,1,0:T(8,128)S(1)}, f32[4,2,8,128]{3,2,1,0:T(8,128)S(1)}, u32[]{:S(2)}, u32[]{:S(2)}) collective-permute-start(f32[4,2,8,128]{3,2,1,0:T(8,128)S(1)} %pad_maximum_fusion.18), channel_id=1, source_target_pairs={{16,0},{32,16},{48,32},{64,48},{80,64},{96,80},{112,96},{128,112},... | collective-permute-start | bytes 98312 | tf_op jit(solution)/shard_map/ppermute | solution.py:18
  87.8 7.9 %collective-permute-start.8 = (f32[4,8,8,128]{3,2,1,0:T(8,128)S(1)}, f32[4,8,8,128]{3,2,1,0:T(8,128)S(1)}, u32[]{:S(2)}, u32[]{:S(2)}) collective-permute-start(f32[4,8,8,128]{3,2,1,0:T(8,128)S(1)} %pad_maximum_fusion.15), channel_id=1, source_target_pairs={{16,0},{32,16},{48,32},{64,48},{80,64},{96,80},{112,96},{128,112},... | collective-permute-start | bytes 393224 | tf_op jit(solution)/shard_map/ppermute | solution.py:26
  95.8 17.2 %collective-permute-start.10 = (f32[4,2,8,128]{3,2,1,0:T(8,128)S(1)}, f32[4,2,8,128]{3,2,1,0:T(8,128)S(1)}, u32[]{:S(2)}, u32[]{:S(2)}) collective-permute-start(f32[4,2,8,128]{3,2,1,0:T(8,128)S(1)} %slice.661), channel_id=1, source_target_pairs={{0,16},{16,32},{32,48},{48,64},{64,80},{80,96},{96,112},{112,128},... | collective-permute-start | bytes 98312 | tf_op jit(solution)/shard_map/ppermute | solution.py:15
  97.7 15.6 %collective-permute-start.11 = (f32[2,48,2,128]{3,2,1,0:T(2,128)S(1)}, f32[2,48,2,128]{3,2,1,0:T(2,128)S(1)}, u32[]{:S(2)}, u32[]{:S(2)}) collective-permute-start(f32[2,48,2,128]{3,2,1,0:T(2,128)S(1)} %get-tuple-element.10), channel_id=1, source_target_pairs={{0,1},{1,2},{2,3},{3,4},{4,5},{5,6},{6,7},{7,8},{8,9},{9,10},{10,1... | collective-permute-start | bytes 294920 | tf_op jit(solution)/shard_map/ppermute | solution.py:15
  99.7 15.5 %collective-permute-start.12 = (f32[2,48,2,128]{3,2,1,0:T(2,128)S(1)}, f32[2,48,2,128]{3,2,1,0:T(2,128)S(1)}, u32[]{:S(2)}, u32[]{:S(2)}) collective-permute-start(f32[2,48,2,128]{3,2,1,0:T(2,128)S(1)} %get-tuple-element.11), channel_id=1, source_target_pairs={{1,0},{2,1},{3,2},{4,3},{5,4},{6,5},{7,6},{8,7},{9,8},{10,9},{11,1... | collective-permute-start | bytes 294920 | tf_op jit(solution)/shard_map/ppermute | solution.py:18
  115.5 42.1 %copy-start.6 = (f32[48,8,128]{2,1,0:T(8,128)}, f32[48,8,128]{2,1,0:T(8,128)S(1)}, u32[]{:S(2)}) copy-start(f32[48,8,128]{2,1,0:T(8,128)S(1)} %get-tuple-element.4) | copy-start | bytes 589828
  115.9 29.3 %collective-permute-start.14 = (f32[2,8,128]{2,1,0:T(8,128)S(1)}, f32[2,8,128]{2,1,0:T(8,128)S(1)}, u32[]{:S(2)}, u32[]{:S(2)}) collective-permute-start(f32[2,8,128]{2,1,0:T(8,128)S(1)} %get-tuple-element.28), channel_id=1, source_target_pairs={{16,0},{32,16},{48,32},{64,48},{80,64},{96,80},{112,96},{128,112},... | collective-permute-start | bytes 24584 | tf_op jit(solution)/shard_map/ppermute | solution.py:18
  127.3 17.8 %collective-permute-start.13 = (f32[2,8,128]{2,1,0:T(8,128)S(1)}, f32[2,8,128]{2,1,0:T(8,128)S(1)}, u32[]{:S(2)}, u32[]{:S(2)}) collective-permute-start(f32[2,8,128]{2,1,0:T(8,128)S(1)} %get-tuple-element.29), channel_id=1, source_target_pairs={{0,16},{16,32},{32,48},{48,64},{64,80},{80,96},{96,112},{112,128},... | collective-permute-start | bytes 24584 | tf_op jit(solution)/shard_map/ppermute | solution.py:15
  129.4 28.2 %copy-start.5 = (f32[48,8,128]{2,1,0:T(8,128)}, f32[48,8,128]{2,1,0:T(8,128)S(1)}, u32[]{:S(2)}) copy-start(f32[48,8,128]{2,1,0:T(8,128)S(1)} %fusion.46) | copy-start | bytes 589828
  129.4 15.7 %collective-permute-start.16 = (f32[48,2,128]{2,1,0:T(2,128)S(1)}, f32[48,2,128]{2,1,0:T(2,128)S(1)}, u32[]{:S(2)}, u32[]{:S(2)}) collective-permute-start(f32[48,2,128]{2,1,0:T(2,128)S(1)} %get-tuple-element.30), channel_id=1, source_target_pairs={{1,0},{2,1},{3,2},{4,3},{5,4},{6,5},{7,6},{8,7},{9,8},{10,9},{11,1... | collective-permute-start | bytes 147464 | tf_op jit(solution)/shard_map/ppermute | solution.py:18
  142.6 15.0 %collective-permute-start.15 = (f32[48,2,128]{2,1,0:T(2,128)S(1)}, f32[48,2,128]{2,1,0:T(2,128)S(1)}, u32[]{:S(2)}, u32[]{:S(2)}) collective-permute-start(f32[48,2,128]{2,1,0:T(2,128)S(1)} %get-tuple-element.31), channel_id=1, source_target_pairs={{0,1},{1,2},{2,3},{3,4},{4,5},{5,6},{6,7},{7,8},{8,9},{9,10},{10,1... | collective-permute-start | bytes 147464 | tf_op jit(solution)/shard_map/ppermute | solution.py:15
  144.8 12.8 %copy-start.1 = (f32[48,8,128]{2,1,0:T(8,128)}, f32[48,8,128]{2,1,0:T(8,128)S(1)}, u32[]{:S(2)}) copy-start(f32[48,8,128]{2,1,0:T(8,128)S(1)} %fusion.31) | copy-start | bytes 589828
where the time goes:
time: 159 us
  starting transfers between devices  114 us (72%)
  waiting for transfers between devices  33.2 us (21%)
  other arithmetic  5.68 us (4%)
  local copies, waits for them, and re-layouts  4.38 us (3%)
    ppermute x8, starting transfers between devices, extended(): lax.ppermute(lax.slice_in_dim(block, 0, width, axis=dim), axis, backward)  96.9 us
    ppermute x8, waiting for transfers between devices, extended(): lax.ppermute(lax.slice_in_dim(block, block.shape[dim] - width, None, axis...  25.6 us
    ppermute x8, starting transfers between devices, extended(): lax.ppermute(lax.slice_in_dim(block, block.shape[dim] - width, None, axis...  15.4 us
    ppermute x1, waiting for transfers between devices, shifted(): lax.ppermute(value, axis, [(source, source + steps) for source in range(f...  5.87 us
  transfers between devices with their start and end apart: 17, of which 5 were waited for; matrix products, arithmetic and copies ran while one was open for 3% of the time, Pallas kernels for 0%

commit v1 on v0

v1 whole, which is shorter than its diff:
```python
import jax
import jax.numpy as jnp
from jax import lax
from jax.experimental import pallas as pl
from jax.experimental.pallas import tpu as pltpu
from jax.sharding import PartitionSpec as P

MESH = pl.DeviceIdType.MESH
N = 48
H = 8
HALO = 14
SHIFT = 8
BASE = 3
ROWS = 56
FIRST = 40
UP, DOWN = 7, 6


def planes(ref, start, count):
    rows = pl.ds(pl.multiple_of(start * H, H), count * H)
    return ref[rows, :].reshape(count, H, 128)


def put(ref, start, value):
    rows = pl.ds(pl.multiple_of(start * H, H), value.shape[0] * H)
    ref[rows, :] = value.reshape(value.shape[0] * H, 128)


def row(ref, start, k):
    return ref[pl.ds(start * H + k, H, stride=H), :]


def put_row(ref, start, k, value):
    ref[pl.ds(start * H + k, H, stride=H), :] = value


def lat(value, steps):
    return pltpu.roll(value, steps % 128, 2)


def hgt(value, steps):
    return pltpu.roll(value, steps % H, 1)


def central(x, count):
    return 8.0 * (x[3 : 3 + count] - x[1 : 1 + count]) - (x[4 : 4 + count] - x[0:count])


def flows(src, dst, start, count, to, coef):
    press, vert, radial, lateral = src
    new_vert, new_radial, new_lateral = dst
    p = planes(press, start - 1, count + 3)
    u = planes(radial, start - 2, count + 4)
    v = planes(lateral, start - 2, count + 4)
    w = planes(vert, start - 2, count + 4)
    b1, a1, s0, s1, k0, k1, k2, km = (coef[i] for i in range(8))
    here, mid = p[1 : 1 + count], w[2 : 2 + count]
    put(
        new_radial,
        to,
        u[2 : 2 + count]
        - b1 * (27.0 * (p[2 : 2 + count] - here) - (p[3 : 3 + count] - p[0:count]))
        - a1 * central(u, count)
        - (s0 * mid + s1 * hgt(mid, 1)),
    )
    put(
        new_lateral,
        to,
        v[2 : 2 + count]
        - b1 * (27.0 * (lat(here, -1) - here) - (lat(here, -2) - lat(here, 1)))
        - a1 * central(v, count),
    )
    put(
        new_vert,
        to,
        mid
        + (k0 * here - k1 * hgt(here, -1))
        + (k2 * hgt(here, -2) - km * hgt(here, 1))
        - a1 * central(w, count),
    )


def pressures(press, new, dst, start, at, count, to, coef):
    new_vert, new_radial, new_lateral = new
    p = planes(press, start - 2, count + 4)
    u = planes(new_radial, at - 2, count + 3)
    v = planes(new_lateral, at, count)
    w = planes(new_vert, at, count)
    c1, a1, d1, d2, dm = coef[8], coef[1], coef[9], coef[10], coef[11]
    spread = (
        27.0 * (u[2 : 2 + count] - u[1 : 1 + count])
        - (u[3 : 3 + count] - u[0:count])
        + 27.0 * (v - lat(v, 1))
        - (lat(v, -1) - lat(v, 2))
        + (27.0 * w - d1 * hgt(w, 1))
        - (dm * hgt(w, -1) - d2 * hgt(w, 2))
    )
    put(dst, to, p[2 : 2 + count] - c1 * spread - a1 * central(p, count))


def kernel(
    ranges,
    heights,
    press_in,
    vert_in,
    radial_in,
    lateral_in,
    stiff_in,
    buoy_in,
    wind_in,
    press_out,
    vert_out,
    radial_out,
    lateral_out,
    p0,
    w0,
    u0,
    v0,
    p1,
    w1,
    u1,
    v1,
    p2,
    w2,
    u2,
    v2,
    stiff,
    buoy,
    wind,
    coef,
    up_send,
    up_recv,
    down_send,
    down_recv,
    up_more,
    low_more,
    down_more,
    high_more,
    low_w,
    halo,
    local_sem,
    send_sem,
    recv_sem,
):
    r, h = lax.axis_index("range"), lax.axis_index("height")
    first_r, last_r = r == 0, r == ranges - 1
    first_h, last_h = h == 0, h == heights - 1
    left = (lax.rem(r + ranges - 1, ranges), h)
    right = (lax.rem(r + 1, ranges), h)
    below = (r, lax.rem(h + heights - 1, heights))
    above = (r, lax.rem(h + 1, heights))
    no_left, no_right = jnp.logical_not(first_r), jnp.logical_not(last_r)
    no_below, no_above = jnp.logical_not(first_h), jnp.logical_not(last_h)

    barrier = pltpu.get_barrier_semaphore()
    for there, device in ((no_below, below), (no_above, above), (no_right, right)):

        @pl.when(there)
        def _():
            pl.semaphore_signal(barrier, inc=1, device_id=device, device_id_type=MESH)

    whole = pl.ds(0, N * H)
    loads = [
        pltpu.make_async_copy(src, dst, local_sem.at[i])
        for i, (src, dst) in enumerate(
            (
                (buoy_in, buoy),
                (stiff_in, stiff),
                (wind_in, wind),
                (press_in, p0.at[whole]),
                (vert_in, w0.at[whole]),
                (radial_in, u0.at[whole]),
                (lateral_in, v0.at[whole]),
            )
        )
    ]
    for load in loads:
        load.start()
    for load in loads[:3]:
        load.wait()

    k = lax.broadcasted_iota(jnp.int32, (H, 128), 0)
    lane = lax.broadcasted_iota(jnp.int32, (H, 128), 1)
    spread_wind = jnp.broadcast_to(wind[...], (H, 128))
    top = heights * H - 1

    def wind_at(rows):
        chosen = jnp.where(lane == rows, spread_wind, 0.0)
        return jnp.broadcast_to(jnp.sum(chosen, axis=1, keepdims=True), (H, 128))

    def shear_at(rows):
        upper = wind_at(jnp.where(rows < top, rows + 1, top))
        lower = wind_at(jnp.where(rows > 0, rows - 1, 0))
        return 0.5 * (upper - lower)

    mine = k + h * H
    b24, c24 = buoy[...] * (1.0 / 24.0), stiff[...] * (1.0 / 24.0)
    a12 = wind_at(mine) * (1.0 / 12.0)
    half_shear = 0.5 * shear_at(mine)
    b27 = b24 * 27.0
    full = jnp.full((H, 128), 27.0, jnp.float32)
    one = jnp.full((H, 128), 1.0, jnp.float32)
    for i, value in enumerate(
        (
            b24,
            a12,
            half_shear,
            jnp.where(k > 0, half_shear, 0.0),
            b27,
            jnp.where(k < H - 1, b27, 0.0),
            jnp.where(k < H - 2, b24, 0.0),
            jnp.where(k > 0, b24, 0.0),
            c24,
            jnp.where(k > 0, full, 0.0),
            jnp.where(k > 1, one, 0.0),
            jnp.where(k < H - 1, one, 0.0),
        )
    ):
        coef[i] = value
    a_low1 = wind_at(jnp.full((H, 128), -1, jnp.int32) + h * H) * (1.0 / 12.0)
    a_low2 = wind_at(jnp.full((H, 128), -2, jnp.int32) + h * H) * (1.0 / 12.0)
    a_high = wind_at(jnp.full((H, 128), 8, jnp.int32) + h * H) * (1.0 / 12.0)
    s_high = 0.5 * shear_at(jnp.full((H, 128), 8, jnp.int32) + h * H)
    s_low = 0.5 * shear_at(jnp.full((H, 128), 0, jnp.int32) + h * H)

    up_more[pl.ds(0, H), :] = b24
    down_more[pl.ds(0, H), :] = b24
    up_more[pl.ds(H, H), :] = c24
    down_more[pl.ds(H, H), :] = c24

    def free_flows(start, step, times):
        def body(j, carry):
            at = start + step * j
            flows((p0, w0, u0, v0), (w1, u1, v1), at, step, at, coef)
            return carry

        lax.fori_loop(0, times, body, 0)

    def free_pressures(start, step, times):
        def body(j, carry):
            at = start + step * j
            pressures(p0, (w1, u1, v1), p1, at, at, step, at, coef)
            return carry

        lax.fori_loop(0, times, body, 0)

    def pack(first, last):
        def body(j, carry):
            at = BASE + H * j
            to = pl.ds(pl.multiple_of(j * H, H), H)
            for q, (ref, height) in enumerate(
                ((p0, 7), (w0, 7), (w1, 7), (w1, 6), (p1, 7), (p1, 6), (p1, 5))
            ):
                up_send[q, to, :] = row(ref, at, height)
            for q, (ref, height) in enumerate(
                ((p0, 0), (p0, 1), (w1, 0), (p1, 0), (p1, 1), (p1, 2))
            ):
                down_send[q, to, :] = row(ref, at, height)
            return carry

        lax.fori_loop(first, last, body, 0)

    def remote(src, dst, i, device):
        return pltpu.make_async_remote_copy(
            src_ref=src,
            dst_ref=dst,
            send_sem=send_sem.at[i],
            recv_sem=recv_sem.at[i],
            device_id=device,
            device_id_type=MESH,
        )

    early, late = pl.ds(0, FIRST), pl.ds(FIRST, ROWS - FIRST)
    head, tail = pl.ds(0, HALO * H), pl.ds(N * H, HALO * H)
    ups = [
        remote(up_send.at[:, early], up_recv.at[:, early], 0, above),
        remote(up_send.at[:, late], up_recv.at[:, late], 1, above),
        remote(up_more, low_more, 2, above),
    ]
    downs = [
        remote(down_send.at[:, early], down_recv.at[:, early], 3, below),
        remote(down_send.at[:, late], down_recv.at[:, late], 4, below),
        remote(down_more, high_more, 5, below),
    ]
    lefts = [
        remote(src.at[head], dst.at[tail], 6 + i, left)
        for i, (src, dst) in enumerate(
            ((press_in, p0), (radial_in, u0), (vert_in, w0), (lateral_in, v0))
        )
    ]

    for load in loads[3:]:
        load.wait()
    free_flows(BASE, 6, 7)
    free_pressures(BASE, 5, 8)
    pack(0, FIRST // H)

    peers = sum(there.astype(jnp.int32) for there in (no_below, no_above, no_left))
    pl.semaphore_wait(barrier, peers)

    pl.when(no_above)(ups[0].start)
    pl.when(no_below)(downs[0].start)

    @pl.when(no_left)
    def _():
        for copy in lefts:
            copy.start()

    nothing = jnp.zeros((HALO * H, 128), jnp.float32)

    @pl.when(last_r)
    def _():
        for ref in (p0, u0, w0, v0):
            ref[tail, :] = nothing

    @pl.when(no_right)
    def _():
        for copy in lefts:
            copy.wait_recv()

    free_flows(45, 5, 3)

    def clear_after():
        for ref in (u1, v1, w1, p1):
            ref[pl.ds(N * H, 12 * H), :] = jnp.zeros((12 * H, 128), jnp.float32)

    pl.when(last_r)(clear_after)
    free_pressures(43, 4, 4)
    pl.when(last_r)(clear_after)
    pack(FIRST // H, ROWS // H)
    last = row(w0, BASE + ROWS - H + 1, 7)
    up_more[pl.ds(2 * H, H), :] = last

    @pl.when(no_above)
    def _():
        ups[1].start()
        ups[2].start()

    @pl.when(no_below)
    def _():
        downs[1].start()
        downs[2].start()

    @pl.when(no_below)
    def _():
        for copy in ups:
            copy.wait_recv()

    @pl.when(no_above)
    def _():
        for copy in downs:
            copy.wait_recv()

    @pl.when(first_h)
    def _():
        up_recv[...] = jnp.zeros(up_recv.shape, jnp.float32)
        low_more[...] = jnp.zeros(low_more.shape, jnp.float32)

    @pl.when(last_h)
    def _():
        down_recv[...] = jnp.zeros(down_recv.shape, jnp.float32)
        high_more[...] = jnp.zeros(high_more.shape, jnp.float32)

    def line(ref, i):
        return jnp.broadcast_to(ref[pl.ds(i, 1), :], (H, 128))

    def own(ref, i):
        return jnp.broadcast_to(ref[i : i + 1, :], (H, 128))

    low_w[pl.ds(0, H), :] = jnp.zeros((H, 128), jnp.float32)
    low_w[pl.ds(H, ROWS), :] = up_recv[1]
    low_w[pl.ds(H + ROWS, H), :] = jnp.broadcast_to(
        low_more[pl.ds(3 * H - 1, 1), :], (H, 128)
    )
    first_plane = jnp.where(first_r, SHIFT, 0)
    after_plane = jnp.where(last_r, N, 2 * N)

    def changes(low_p, low_w, high_p, high_p2):
        d0 = own(b24, 0) * low_p * -1.0
        d7 = own(b24, 7) * (high_p2 - 27.0 * high_p)
        d6 = own(b24, 6) * high_p
        return d0, d6, d7

    def correct_pressure(ref, at, du, d0, d6, d7, low1, low2, high):
        for i, add in (
            (0, du + 27.0 * (d0 - low1) + low2),
            (1, low1 - 27.0 * d0),
            (2, d0),
            (5, -d6),
            (6, 27.0 * d6 - d7),
            (7, 27.0 * (d7 - d6) - high),
        ):
            put_row(ref, at, i, row(ref, at, i) - own(c24, i) * add)

    def correct_first(j, carry):
        at = BASE + H * j
        here = pl.ds(pl.multiple_of(j * H, H), H)
        low_p0, low_w1, low_w2 = up_recv[0, here, :], up_recv[2, here, :], up_recv[3, here, :]
        high_p0, high_p0b = down_recv[0, here, :], down_recv[1, here, :]
        wl = [low_w[pl.ds(j * H + H + s, H), :] for s in (-2, -1, 0, 1)]
        wt = [row(w0, at + s, 7) for s in (-2, -1, 0, 1)]
        own_p0, own_p1, own_p7 = row(p0, at, 0), row(p0, at, 1), row(p0, at, 7)
        e1 = line(low_more, 7) * (own_p1 - 27.0 * own_p0)
        e2 = line(low_more, 6) * own_p0
        e8 = line(high_more, 0) * own_p7 * -1.0
        low_w1, low_w2 = low_w1 + e1, low_w2 + e2
        high_w = down_recv[2, here, :] + e8
        d0, d6, d7 = changes(low_p0, None, high_p0, high_p0b)
        new0, new6, new7 = row(w1, at, 0) + d0, row(w1, at, 6) + d6, row(w1, at, 7) + d7
        put_row(w1, at, 0, new0)
        put_row(w1, at, 6, new6)
        put_row(w1, at, 7, new7)
        put_row(u1, at, 0, row(u1, at, 0) - s_low * wl[2])
        du = -s_low * (27.0 * (wl[2] - wl[1]) - (wl[3] - wl[0]))
        correct_pressure(p1, at, du, d0, d6, d7, low_w1, low_w2, high_w)
        du_high = -s_high * (27.0 * (wt[2] - wt[1]) - (wt[3] - wt[0]))
        low_p1 = up_recv[4, here, :] - line(low_more, H + 7) * (27.0 * (e1 - e2) - new0)
        low_p2 = up_recv[5, here, :] - line(low_more, H + 6) * (27.0 * e2 - e1)
        low_p3 = up_recv[6, here, :] + line(low_more, H + 5) * e2
        high_p1 = down_recv[3, here, :] - line(high_more, H) * (
            du_high + 27.0 * (e8 - new7) + new6
        )
        high_p2 = down_recv[4, here, :] - line(high_more, H + 1) * (new7 - 27.0 * e8)
        high_p3 = down_recv[5, here, :] - line(high_more, H + 2) * e8
        plane = k + at
        keep = jnp.logical_and(plane >= first_plane, plane < after_plane)
        for i, value in enumerate(
            (low_w1, low_w2, low_p1, low_p2, low_p3, high_w, high_p1, high_p2, high_p3)
        ):
            halo[i, here, :] = jnp.where(keep, value, 0.0)
        return carry

    lax.fori_loop(0, ROWS // H, correct_first, 0)

    @pl.when(first_r)
    def _():
        for ref in (u1, v1, w1, p1):
            ref[pl.ds(0, SHIFT * H), :] = jnp.zeros((SHIFT * H, 128), jnp.float32)

    pl.when(last_r)(clear_after)

    def second_flows(j, carry):
        at = 8 * j
        flows((p1, w1, u1, v1), (w2, u2, v2), at + SHIFT, 8, at + 2, coef)
        return carry

    lax.fori_loop(0, N // 8, second_flows, 0)
    flows((p1, w1, u1, v1), (w2, u2, v2), SHIFT - 2, 2, 0, coef)
    flows((p1, w1, u1, v1), (w2, u2, v2), SHIFT + N, 1, N + 2, coef)

    @pl.when(first_r)
    def _():
        u2[pl.ds(0, 2 * H), :] = jnp.zeros((2 * H, 128), jnp.float32)

    def second_pressures(j, carry):
        at = 8 * j
        pressures(p1, (w2, u2, v2), p2, at + SHIFT, at + 2, 8, at, coef)
        return carry

    lax.fori_loop(0, N // 8, second_pressures, 0)

    def correct_second(j, carry):
        at = H * j
        off = at + SHIFT - BASE

        def rows_of(i, s=0):
            return halo[i, pl.ds(off + s, H), :]

        def across(i):
            return 8.0 * (rows_of(i, 1) - rows_of(i, -1)) - (rows_of(i, 2) - rows_of(i, -2))

        low_w1, low_w2, low_p1, low_p2, low_p3, high_w, high_p1, high_p2, high_p3 = (
            rows_of(i) for i in range(9)
        )
        own_p0, own_p1, own_p7 = (row(p1, at + SHIFT, i) for i in (0, 1, 7))
        d0, d6, d7 = changes(low_p1, None, high_p1, high_p2)
        put_row(w2, at + 2, 0, row(w2, at + 2, 0) + d0)
        put_row(w2, at + 2, 6, row(w2, at + 2, 6) + d6)
        put_row(w2, at + 2, 7, row(w2, at + 2, 7) + d7)
        put_row(u2, at + 2, 0, row(u2, at + 2, 0) - s_low * low_w1)
        du = -s_low * (
            27.0 * (low_w1 - rows_of(0, -1)) - (rows_of(0, 1) - rows_of(0, -2))
        )
        new1 = (
            low_w1
            - line(low_more, 7) * (27.0 * (own_p0 - low_p1) - (own_p1 - low_p2))
            - a_low1 * across(0)
        )
        new2 = (
            low_w2
            - line(low_more, 6) * (27.0 * (low_p1 - low_p2) - (own_p0 - low_p3))
            - a_low2 * across(1)
        )
        new8 = (
            high_w
            - line(high_more, 0) * (27.0 * (high_p2 - high_p1) - (high_p3 - own_p7))
            - a_high * across(5)
        )
        correct_pressure(p2, at, du, d0, d6, d7, new1, new2, new8)
        return carry

    lax.fori_loop(0, N // H, correct_second, 0)

    inner = pl.ds(2 * H, N * H)
    stores = [
        pltpu.make_async_copy(src, dst, local_sem.at[i])
        for i, (src, dst) in enumerate(
            (
                (p2, press_out),
                (w2.at[inner], vert_out),
                (u2.at[inner], radial_out),
                (v2.at[inner], lateral_out),
            )
        )
    ]
    for store in stores:
        store.start()

    @pl.when(no_above)
    def _():
        for copy in ups:
            copy.wait_send()

    @pl.when(no_below)
    def _():
        for copy in downs:
            copy.wait_send()

    @pl.when(no_left)
    def _():
        for copy in lefts:
            copy.wait_send()

    for store in stores:
        store.wait()


def solution(mesh):
    ranges, heights = mesh.shape["range"], mesh.shape["height"]

    def on_device(press, vert, radial, lateral, stiff, buoy, wind):
        def field(count):
            return pltpu.VMEM((count * H, 128), jnp.float32)

        flat = [x.reshape(N * H, 128) for x in (press, vert, radial, lateral)]
        out = pl.pallas_call(
            lambda *refs: kernel(ranges, heights, *refs),
            out_shape=[jax.ShapeDtypeStruct((N * H, 128), jnp.float32)] * 4,
            in_specs=[pl.BlockSpec(memory_space=pl.ANY)] * 7,
            out_specs=[pl.BlockSpec(memory_space=pl.ANY)] * 4,
            scratch_shapes=[field(64)] * 8
            + [field(N), field(N + 4), field(N + 4), field(N + 4)]
            + [
                field(1),
                field(1),
                pltpu.VMEM((1, 128), jnp.float32),
                pltpu.VMEM((12, H, 128), jnp.float32),
                pltpu.VMEM((UP, ROWS, 128), jnp.float32),
                pltpu.VMEM((UP, ROWS, 128), jnp.float32),
                pltpu.VMEM((DOWN, ROWS, 128), jnp.float32),
                pltpu.VMEM((DOWN, ROWS, 128), jnp.float32),
                field(3),
                field(3),
                field(2),
                field(2),
                pltpu.VMEM((ROWS + 2 * H, 128), jnp.float32),
                pltpu.VMEM((9, ROWS, 128), jnp.float32),
                pltpu.SemaphoreType.DMA((7,)),
                pltpu.SemaphoreType.DMA((10,)),
                pltpu.SemaphoreType.DMA((10,)),
            ],
            compiler_params=pltpu.CompilerParams(
                collective_id=0, has_side_effects=True, vmem_limit_bytes=32 * 2**20
            ),
        )(*flat, stiff, buoy, wind.reshape(1, 128))
        return tuple(x.reshape(N, H, 128) for x in out)

    field_spec = P("range", "height", None)
    return jax.shard_map(
        on_device,
        mesh=mesh,
        in_specs=(field_spec,) * 4 + (P("height", None), P("height", None), P()),
        out_specs=(field_spec,) * 4,
        check_vma=False,
    )
```

time: 159 us -> 51.5 us (0.32)
  the two profiles are of different devices: /device:TPU:10 before, /device:TPU:47 now
where the time goes in v1:
time: 51.5 us; the launch traced here: 51.2 us
  Pallas kernels  43.5 us (84%)
  local copies, waits for them, and re-layouts  7.1 us (14%)
  between operations  0.67 us (1%)
    pallas_call x1, Pallas kernels, on_device(): pl.pallas_call(lambda *refs: kernel(ranges, heights, *refs), out_shape=[j...  43.5 us
    unnamed x18, local copies, waits for them, and re-layouts  7.1 us

profile of v1, /device:TPU:47, one launch (start us, length us, event | category | flops | bytes accessed | tf_op | source)
XLA Modules:
  0.0 51.2 jit_solution(3300770540551870411)
XLA Ops:
  0.6 0.0 copy-start.5
  0.6 0.0 copy-start.4
  0.7 0.0 copy-start.6
  0.7 0.7 %copy-done.5 = f32[8,128]{1,0:T(8,128)S(1)} copy-done((f32[8,128]{1,0:T(8,128)S(1)}, f32[8,128]{1,0:T(8,128)}, u32[]{:S(2)}) %copy-start.5) | copy-done | bytes 4120
  1.3 0.0 copy-done.4
  1.3 0.0 copy-done.6
  1.3 0.0 copy-start
  1.3 0.9 %copy-done = f32[48,8,128]{2,1,0:T(8,128)S(1)} copy-done((f32[48,8,128]{2,1,0:T(8,128)S(1)}, f32[48,8,128]{2,1,0:T(8,128)}, u32[]{:S(2)}) %copy-start) | copy-done | bytes 196632
  2.3 0.0 copy-start.1
  2.3 0.9 %copy-done.1 = f32[48,8,128]{2,1,0:T(8,128)S(1)} copy-done((f32[48,8,128]{2,1,0:T(8,128)S(1)}, f32[48,8,128]{2,1,0:T(8,128)}, u32[]{:S(2)}) %copy-start.1) | copy-done | bytes 196632
  3.2 0.0 copy-start.2
  3.2 0.9 %copy-done.2 = f32[48,8,128]{2,1,0:T(8,128)S(1)} copy-done((f32[48,8,128]{2,1,0:T(8,128)S(1)}, f32[48,8,128]{2,1,0:T(8,128)}, u32[]{:S(2)}) %copy-start.2) | copy-done | bytes 196632
  4.1 0.0 copy-start.3
  4.1 0.9 %copy-done.3 = f32[48,8,128]{2,1,0:T(8,128)S(1)} copy-done((f32[48,8,128]{2,1,0:T(8,128)S(1)}, f32[48,8,128]{2,1,0:T(8,128)}, u32[]{:S(2)}) %copy-start.3) | copy-done | bytes 196632
  5.0 43.5 %shard_map.102 = (f32[384,128]{1,0:T(8,128)S(1)}, f32[384,128]{1,0:T(8,128)S(1)}, f32[384,128]{1,0:T(8,128)S(1)}, f32[384,128]{1,0:T(8,128)S(1)}) custom-call(f32[384,128]{1,0:T(8,128)S(1)} %bitcast.13, f32[384,128]{1,0:T(8,128)S(1)} %bitcast.14, f32[384,128]{1,0:T(8,128)S(1)} %bitcast.15, f32[384,128]{1,0:T(8,128)S(1)} %bitcast.16, f32[8,128]{1,0:T(8,128)S(1)} %copy-done.4, ...), custom_call_target="tpu_custom_call" | custom-call | tf_op jit(solution)/shard_map/pallas_call | solution.py:546
  48.5 0.7 %copy.15 = f32[48,8,128]{2,1,0:T(8,128)} copy(f32[48,8,128]{2,1,0:T(8,128)S(1)} %bitcast.12) | data formatting | bytes 393216
  49.2 0.7 %copy.16 = f32[48,8,128]{2,1,0:T(8,128)} copy(f32[48,8,128]{2,1,0:T(8,128)S(1)} %bitcast.11) | data formatting | bytes 393216
  49.9 0.7 %copy.17 = f32[48,8,128]{2,1,0:T(8,128)} copy(f32[48,8,128]{2,1,0:T(8,128)S(1)} %bitcast.10) | data formatting | bytes 393216
  50.6 0.7 %copy.18 = f32[48,8,128]{2,1,0:T(8,128)} copy(f32[48,8,128]{2,1,0:T(8,128)S(1)} %bitcast.9) | data formatting | bytes 393216
Async XLA Ops:
  0.6 0.7 %copy-start.5 = (f32[8,128]{1,0:T(8,128)S(1)}, f32[8,128]{1,0:T(8,128)}, u32[]{:S(2)}) copy-start(f32[8,128]{1,0:T(8,128)} %refs_5_.1) | copy-start | bytes 12292
  0.6 0.7 %copy-start.4 = (f32[8,128]{1,0:T(8,128)S(1)}, f32[8,128]{1,0:T(8,128)}, u32[]{:S(2)}) copy-start(f32[8,128]{1,0:T(8,128)} %refs_4_.1) | copy-start | bytes 12292
  0.7 0.7 %copy-start.6 = (f32[128]{0:T(128)S(1)}, f32[128]{0:T(128)}, u32[]{:S(2)}) copy-start(f32[128]{0:T(128)} %param.13) | copy-start | bytes 1540
  1.3 0.9 %copy-start = (f32[48,8,128]{2,1,0:T(8,128)S(1)}, f32[48,8,128]{2,1,0:T(8,128)}, u32[]{:S(2)}) copy-start(f32[48,8,128]{2,1,0:T(8,128)} %param.7) | copy-start | bytes 589828
  2.3 0.9 %copy-start.1 = (f32[48,8,128]{2,1,0:T(8,128)S(1)}, f32[48,8,128]{2,1,0:T(8,128)}, u32[]{:S(2)}) copy-start(f32[48,8,128]{2,1,0:T(8,128)} %param.8) | copy-start | bytes 589828
  3.2 0.9 %copy-start.2 = (f32[48,8,128]{2,1,0:T(8,128)S(1)}, f32[48,8,128]{2,1,0:T(8,128)}, u32[]{:S(2)}) copy-start(f32[48,8,128]{2,1,0:T(8,128)} %param.9) | copy-start | bytes 589828
  4.1 0.9 %copy-start.3 = (f32[48,8,128]{2,1,0:T(8,128)S(1)}, f32[48,8,128]{2,1,0:T(8,128)}, u32[]{:S(2)}) copy-start(f32[48,8,128]{2,1,0:T(8,128)} %param.10) | copy-start | bytes 589828

commit v2 on v1

--- a/solution.py
+++ b/solution.py
@@ -98,7 +98,39 @@
     put(dst, to, p[2 : 2 + count] - c1 * spread - a1 * central(p, count))
 
 
-def kernel(
+def line(ref, i):
+    return jnp.broadcast_to(ref[pl.ds(i, 1), :], (H, 128))
+
+
+def changes(coef, low_p, high_p, high_p2):
+    b24 = coef.at[0]
+    return (
+        -line(b24, 0) * low_p,
+        line(b24, 6) * high_p,
+        line(b24, 7) * (high_p2 - 27.0 * high_p),
+    )
+
+
+def correct_pressure(ref, at, coef, du, d0, d6, d7, low1, low2, high):
+    c24 = coef.at[8]
+    for i, add in (
+        (0, du + 27.0 * (d0 - low1) + low2),
+        (1, low1 - 27.0 * d0),
+        (2, d0),
+        (5, -d6),
+        (6, 27.0 * d6 - d7),
+        (7, 27.0 * (d7 - d6) - high),
+    ):
+        put_row(ref, at, i, row(ref, at, i) - line(c24, i) * add)
+
+
+def add_row(ref, at, i, value):
+    new = row(ref, at, i) + value
+    put_row(ref, at, i, new)
+    return new
+
+
+def first_step(
     ranges,
     heights,
     press_in,
@@ -108,39 +140,32 @@
     stiff_in,
     buoy_in,
     wind_in,
-    press_out,
-    vert_out,
-    radial_out,
-    lateral_out,
+    p1,
+    w1,
+    u1,
+    v1,
+    halo,
+    coef,
+    low_more,
+    high_more,
     p0,
     w0,
     u0,
     v0,
-    p1,
-    w1,
-    u1,
-    v1,
-    p2,
-    w2,
-    u2,
-    v2,
     stiff,
     buoy,
     wind,
-    coef,
     up_send,
     up_recv,
     down_send,
     down_recv,
     up_more,
-    low_more,
     down_more,
-    high_more,
     low_w,
-    halo,
     local_sem,
     send_sem,
     recv_sem,
+    ready,
 ):
     r, h = lax.axis_index("range"), lax.axis_index("height")
     first_r, last_r = r == 0, r == ranges - 1
@@ -151,9 +176,21 @@
     above = (r, lax.rem(h + 1, heights))
     no_left, no_right = jnp.logical_not(first_r), jnp.logical_not(last_r)
     no_below, no_above = jnp.logical_not(first_h), jnp.logical_not(last_h)
+    odd = lax.rem(h, 2) == 1
+    is_late = lax.rem(h // 2, 2) == 1
+    is_early = jnp.logical_not(is_late)
+    even = jnp.logical_not(odd)
+    far_up, far_down = jnp.logical_and(odd, no_above), jnp.logical_and(even, no_below)
+    near_up, near_down = jnp.logical_and(even, no_above), jnp.logical_and(odd, no_below)
 
     barrier = pltpu.get_barrier_semaphore()
-    for there, device in ((no_below, below), (no_above, above), (no_right, right)):
+    for there, device in (
+        (no_right, right),
+        (near_up, above),
+        (near_down, below),
+        (jnp.logical_and(is_early, far_up), above),
+        (jnp.logical_and(is_early, far_down), below),
+    ):
 
         @pl.when(there)
         def _():
@@ -176,6 +213,54 @@
     ]
     for load in loads:
         load.start()
+    def remote(src, dst, i, device):
+        return pltpu.make_async_remote_copy(
+            src_ref=src,
+            dst_ref=dst,
+            send_sem=send_sem.at[i],
+            recv_sem=recv_sem.at[i],
+            device_id=device,
+            device_id_type=MESH,
+        )
+
+    early, late = pl.ds(0, FIRST), pl.ds(FIRST, ROWS - FIRST)
+    head, tail = pl.ds(0, HALO * H), pl.ds(N * H, HALO * H)
+    ups = [
+        remote(up_send.at[:, early], up_recv.at[:, early], 0, above),
+        remote(up_send.at[:, late], up_recv.at[:, late], 1, above),
+        remote(up_more, low_more, 2, above),
+    ]
+    downs = [
+        remote(down_send.at[:, early], down_recv.at[:, early], 3, below),
+        remote(down_send.at[:, late], down_recv.at[:, late], 4, below),
+        remote(down_more, high_more, 5, below),
+    ]
+    lefts = [
+        remote(src.at[head], dst.at[tail], 6 + i, left)
+        for i, (src, dst) in enumerate(
+            ((press_in, p0), (radial_in, u0), (vert_in, w0), (lateral_in, v0))
+        )
+    ]
+
+    late_far = jnp.logical_and(is_late, jnp.logical_or(far_up, far_down))
+    early_far = jnp.logical_and(is_early, jnp.logical_or(far_up, far_down))
+    peers = sum(
+        there.astype(jnp.int32)
+        for there in (no_left, jnp.logical_or(near_up, near_down), late_far)
+    )
+    pl.semaphore_wait(barrier, peers)
+
+    for there, device in ((far_up, above), (far_down, below)):
+
+        @pl.when(jnp.logical_and(is_late, there))
+        def _():
+            pl.semaphore_signal(ready, inc=1, device_id=device, device_id_type=MESH)
+
+    @pl.when(no_left)
+    def _():
+        for copy in lefts:
+            copy.start()
+
     for load in loads[:3]:
         load.wait()
 
@@ -217,11 +302,11 @@
         )
     ):
         coef[i] = value
-    a_low1 = wind_at(jnp.full((H, 128), -1, jnp.int32) + h * H) * (1.0 / 12.0)
-    a_low2 = wind_at(jnp.full((H, 128), -2, jnp.int32) + h * H) * (1.0 / 12.0)
-    a_high = wind_at(jnp.full((H, 128), 8, jnp.int32) + h * H) * (1.0 / 12.0)
-    s_high = 0.5 * shear_at(jnp.full((H, 128), 8, jnp.int32) + h * H)
-    s_low = 0.5 * shear_at(jnp.full((H, 128), 0, jnp.int32) + h * H)
+    for i, outside in enumerate((-1, -2, H)):
+        coef[12 + i] = wind_at(jnp.zeros_like(k) + (h * H + outside)) * (1.0 / 12.0)
+    s_low = 0.5 * shear_at(jnp.zeros_like(k) + h * H)
+    s_high = 0.5 * shear_at(jnp.zeros_like(k) + (h * H + H))
+    coef[15] = s_low
 
     up_more[pl.ds(0, H), :] = b24
     down_more[pl.ds(0, H), :] = b24
@@ -260,51 +345,19 @@
 
         lax.fori_loop(first, last, body, 0)
 
-    def remote(src, dst, i, device):
-        return pltpu.make_async_remote_copy(
-            src_ref=src,
-            dst_ref=dst,
-            send_sem=send_sem.at[i],
-            recv_sem=recv_sem.at[i],
-            device_id=device,
-            device_id_type=MESH,
-        )
-
-    early, late = pl.ds(0, FIRST), pl.ds(FIRST, ROWS - FIRST)
-    head, tail = pl.ds(0, HALO * H), pl.ds(N * H, HALO * H)
-    ups = [
-        remote(up_send.at[:, early], up_recv.at[:, early], 0, above),
-        remote(up_send.at[:, late], up_recv.at[:, late], 1, above),
-        remote(up_more, low_more, 2, above),
-    ]
-    downs = [
-        remote(down_send.at[:, early], down_recv.at[:, early], 3, below),
-        remote(down_send.at[:, late], down_recv.at[:, late], 4, below),
-        remote(down_more, high_more, 5, below),
-    ]
-    lefts = [
-        remote(src.at[head], dst.at[tail], 6 + i, left)
-        for i, (src, dst) in enumerate(
-            ((press_in, p0), (radial_in, u0), (vert_in, w0), (lateral_in, v0))
-        )
-    ]
-
     for load in loads[3:]:
         load.wait()
     free_flows(BASE, 6, 7)
     free_pressures(BASE, 5, 8)
     pack(0, FIRST // H)
 
-    peers = sum(there.astype(jnp.int32) for there in (no_below, no_above, no_left))
-    pl.semaphore_wait(barrier, peers)
-
-    pl.when(no_above)(ups[0].start)
-    pl.when(no_below)(downs[0].start)
-
-    @pl.when(no_left)
-    def _():
-        for copy in lefts:
-            copy.start()
+    def send(i):
+        for there, copies in ((far_up, ups), (far_down, downs)):
+            pl.when(jnp.logical_and(is_late, there))(copies[i].start)
+        for there, copies in ((near_up, ups), (near_down, downs)):
+            pl.when(there)(copies[i].start)
+
+    send(0)
 
     nothing = jnp.zeros((HALO * H, 128), jnp.float32)
 
@@ -331,15 +384,19 @@
     last = row(w0, BASE + ROWS - H + 1, 7)
     up_more[pl.ds(2 * H, H), :] = last
 
-    @pl.when(no_above)
-    def _():
-        ups[1].start()
-        ups[2].start()
-
-    @pl.when(no_below)
-    def _():
-        downs[1].start()
-        downs[2].start()
+    send(1)
+    send(2)
+
+    @pl.when(early_far)
+    def _():
+        pl.semaphore_wait(ready, 1)
+
+    for there, copies in ((far_up, ups), (far_down, downs)):
+
+        @pl.when(jnp.logical_and(is_early, there))
+        def _():
+            for copy in copies:
+                copy.start()
 
     @pl.when(no_below)
     def _():
@@ -360,12 +417,6 @@
     def _():
         down_recv[...] = jnp.zeros(down_recv.shape, jnp.float32)
         high_more[...] = jnp.zeros(high_more.shape, jnp.float32)
-
-    def line(ref, i):
-        return jnp.broadcast_to(ref[pl.ds(i, 1), :], (H, 128))
-
-    def own(ref, i):
-        return jnp.broadcast_to(ref[i : i + 1, :], (H, 128))
 
     low_w[pl.ds(0, H), :] = jnp.zeros((H, 128), jnp.float32)
     low_w[pl.ds(H, ROWS), :] = up_recv[1]
@@ -374,23 +425,6 @@
     )
     first_plane = jnp.where(first_r, SHIFT, 0)
     after_plane = jnp.where(last_r, N, 2 * N)
-
-    def changes(low_p, low_w, high_p, high_p2):
-        d0 = own(b24, 0) * low_p * -1.0
-        d7 = own(b24, 7) * (high_p2 - 27.0 * high_p)
-        d6 = own(b24, 6) * high_p
-        return d0, d6, d7
-
-    def correct_pressure(ref, at, du, d0, d6, d7, low1, low2, high):
-        for i, add in (
-            (0, du + 27.0 * (d0 - low1) + low2),
-            (1, low1 - 27.0 * d0),
-            (2, d0),
-            (5, -d6),
-            (6, 27.0 * d6 - d7),
-            (7, 27.0 * (d7 - d6) - high),
-        ):
-            put_row(ref, at, i, row(ref, at, i) - own(c24, i) * add)
 
     def correct_first(j, carry):
         at = BASE + H * j
@@ -405,14 +439,11 @@
         e8 = line(high_more, 0) * own_p7 * -1.0
         low_w1, low_w2 = low_w1 + e1, low_w2 + e2
         high_w = down_recv[2, here, :] + e8
-        d0, d6, d7 = changes(low_p0, None, high_p0, high_p0b)
-        new0, new6, new7 = row(w1, at, 0) + d0, row(w1, at, 6) + d6, row(w1, at, 7) + d7
-        put_row(w1, at, 0, new0)
-        put_row(w1, at, 6, new6)
-        put_row(w1, at, 7, new7)
-        put_row(u1, at, 0, row(u1, at, 0) - s_low * wl[2])
+        d0, d6, d7 = changes(coef, low_p0, high_p0, high_p0b)
+        new0, new6, new7 = (add_row(w1, at, i, d) for i, d in ((0, d0), (6, d6), (7, d7)))
+        add_row(u1, at, 0, -s_low * wl[2])
         du = -s_low * (27.0 * (wl[2] - wl[1]) - (wl[3] - wl[0]))
-        correct_pressure(p1, at, du, d0, d6, d7, low_w1, low_w2, high_w)
+        correct_pressure(p1, at, coef, du, d0, d6, d7, low_w1, low_w2, high_w)
         du_high = -s_high * (27.0 * (wt[2] - wt[1]) - (wt[3] - wt[0]))
         low_p1 = up_recv[4, here, :] - line(low_more, H + 7) * (27.0 * (e1 - e2) - new0)
         low_p2 = up_recv[5, here, :] - line(low_more, H + 6) * (27.0 * e2 - e1)
@@ -439,6 +470,42 @@
 
     pl.when(last_r)(clear_after)
 
+    @pl.when(no_above)
+    def _():
+        for copy in ups:
+            copy.wait_send()
+
+    @pl.when(no_below)
+    def _():
+        for copy in downs:
+            copy.wait_send()
+
+    @pl.when(no_left)
+    def _():
+        for copy in lefts:
+            copy.wait_send()
+
+
+def second_step(
+    p1,
+    w1,
+    u1,
+    v1,
+    halo,
+    coef,
+    low_more,
+    high_more,
+    press_out,
+    vert_out,
+    radial_out,
+    lateral_out,
+    p2,
+    w2,
+    u2,
+    v2,
+    sems,
+):
+    first_r = lax.axis_index("range") == 0
     def second_flows(j, carry):
         at = 8 * j
         flows((p1, w1, u1, v1), (w2, u2, v2), at + SHIFT, 8, at + 2, coef)
@@ -473,37 +540,36 @@
             rows_of(i) for i in range(9)
         )
         own_p0, own_p1, own_p7 = (row(p1, at + SHIFT, i) for i in (0, 1, 7))
-        d0, d6, d7 = changes(low_p1, None, high_p1, high_p2)
-        put_row(w2, at + 2, 0, row(w2, at + 2, 0) + d0)
-        put_row(w2, at + 2, 6, row(w2, at + 2, 6) + d6)
-        put_row(w2, at + 2, 7, row(w2, at + 2, 7) + d7)
-        put_row(u2, at + 2, 0, row(u2, at + 2, 0) - s_low * low_w1)
-        du = -s_low * (
+        d0, d6, d7 = changes(coef, low_p1, high_p1, high_p2)
+        for i, d in ((0, d0), (6, d6), (7, d7)):
+            add_row(w2, at + 2, i, d)
+        add_row(u2, at + 2, 0, -coef[15] * low_w1)
+        du = -coef[15] * (
             27.0 * (low_w1 - rows_of(0, -1)) - (rows_of(0, 1) - rows_of(0, -2))
         )
         new1 = (
             low_w1
             - line(low_more, 7) * (27.0 * (own_p0 - low_p1) - (own_p1 - low_p2))
-            - a_low1 * across(0)
+            - coef[12] * across(0)
         )
         new2 = (
             low_w2
             - line(low_more, 6) * (27.0 * (low_p1 - low_p2) - (own_p0 - low_p3))
-            - a_low2 * across(1)
+            - coef[13] * across(1)
         )
         new8 = (
             high_w
             - line(high_more, 0) * (27.0 * (high_p2 - high_p1) - (high_p3 - own_p7))
-            - a_high * across(5)
-        )
-        correct_pressure(p2, at, du, d0, d6, d7, new1, new2, new8)
+            - coef[14] * across(5)
+        )
+        correct_pressure(p2, at, coef, du, d0, d6, d7, new1, new2, new8)
         return carry
 
     lax.fori_loop(0, N // H, correct_second, 0)
 
     inner = pl.ds(2 * H, N * H)
     stores = [
-        pltpu.make_async_copy(src, dst, local_sem.at[i])
+        pltpu.make_async_copy(src, dst, sems.at[i])
         for i, (src, dst) in enumerate(
             (
                 (p2, press_out),
@@ -516,21 +582,6 @@
     for store in stores:
         store.start()
 
-    @pl.when(no_above)
-    def _():
-        for copy in ups:
-            copy.wait_send()
-
-    @pl.when(no_below)
-    def _():
-        for copy in downs:
-            copy.wait_send()
-
-    @pl.when(no_left)
-    def _():
-        for copy in lefts:
-            copy.wait_send()
-
     for store in stores:
         store.wait()
 
@@ -543,36 +594,51 @@
             return pltpu.VMEM((count * H, 128), jnp.float32)
 
         flat = [x.reshape(N * H, 128) for x in (press, vert, radial, lateral)]
-        out = pl.pallas_call(
-            lambda *refs: kernel(ranges, heights, *refs),
-            out_shape=[jax.ShapeDtypeStruct((N * H, 128), jnp.float32)] * 4,
-            in_specs=[pl.BlockSpec(memory_space=pl.ANY)] * 7,
-            out_specs=[pl.BlockSpec(memory_space=pl.ANY)] * 4,
-            scratch_shapes=[field(64)] * 8
-            + [field(N), field(N + 4), field(N + 4), field(N + 4)]
+        arguments = [
+            pltpu.with_memory_space_constraint(x, pltpu.HBM)
+            for x in (*flat, stiff, buoy, wind.reshape(1, 128))
+        ]
+        state = pl.pallas_call(
+            lambda *refs: first_step(ranges, heights, *refs),
+            out_shape=[field(64)] * 4
+            + [
+                pltpu.VMEM((9, ROWS, 128), jnp.float32),
+                pltpu.VMEM((16, H, 128), jnp.float32),
+                field(3),
+                field(2),
+            ],
+            in_specs=[pl.BlockSpec(memory_space=pltpu.HBM)] * 7,
+            out_specs=[pl.BlockSpec(memory_space=pltpu.VMEM)] * 8,
+            scratch_shapes=[field(64)] * 4
             + [
                 field(1),
                 field(1),
                 pltpu.VMEM((1, 128), jnp.float32),
-                pltpu.VMEM((12, H, 128), jnp.float32),
                 pltpu.VMEM((UP, ROWS, 128), jnp.float32),
                 pltpu.VMEM((UP, ROWS, 128), jnp.float32),
                 pltpu.VMEM((DOWN, ROWS, 128), jnp.float32),
                 pltpu.VMEM((DOWN, ROWS, 128), jnp.float32),
                 field(3),
-                field(3),
-                field(2),
                 field(2),
                 pltpu.VMEM((ROWS + 2 * H, 128), jnp.float32),
-                pltpu.VMEM((9, ROWS, 128), jnp.float32),
                 pltpu.SemaphoreType.DMA((7,)),
                 pltpu.SemaphoreType.DMA((10,)),
                 pltpu.SemaphoreType.DMA((10,)),
+                pltpu.SemaphoreType.REGULAR,
             ],
             compiler_params=pltpu.CompilerParams(
-                collective_id=0, has_side_effects=True, vmem_limit_bytes=32 * 2**20
+                collective_id=0, has_side_effects=True, vmem_limit_bytes=24 * 2**20
             ),
-        )(*flat, stiff, buoy, wind.reshape(1, 128))
+        )(*arguments)
+        out = pl.pallas_call(
+            second_step,
+            out_shape=[jax.ShapeDtypeStruct((N * H, 128), jnp.float32)] * 4,
+            in_specs=[pl.BlockSpec(memory_space=pltpu.VMEM)] * 8,
+            out_specs=[pl.BlockSpec(memory_space=pltpu.HBM)] * 4,
+            scratch_shapes=[field(N), field(N + 4), field(N + 4), field(N + 4)]
+            + [pltpu.SemaphoreType.DMA((4,))],
+            compiler_params=pltpu.CompilerParams(vmem_limit_bytes=24 * 2**20),
+        )(*state)
         return tuple(x.reshape(N, H, 128) for x in out)
 
     field_spec = P("range", "height", None)

time: 51.5 us -> 39.8 us (0.77)
  the two profiles are of different devices: /device:TPU:47 before, /device:TPU:463 now
where the time goes in v2:
time: 39.8 us; the launch traced here: 39.7 us
  Pallas kernels  39 us (98%)
  between operations  0.64 us (2%)
    pallas_call x1, Pallas kernels, on_device(): pl.pallas_call(lambda *refs: first_step(ranges, heights, *refs), out_shap...  36.7 us
    pallas_call x1, Pallas kernels, on_device(): pl.pallas_call(second_step, out_shape=[jax.ShapeDtypeStruct((N * H, 128),...  2.35 us

profile of v2, /device:TPU:463, one launch (start us, length us, event | category | flops | bytes accessed | tf_op | source)
XLA Modules:
  0.0 39.7 jit_solution(3575815341669837690)
XLA Ops:
  0.6 36.7 %shard_map.102 = (f32[512,128]{1,0:T(8,128)S(1)}, f32[512,128]{1,0:T(8,128)S(1)}, f32[512,128]{1,0:T(8,128)S(1)}, f32[512,128]{1,0:T(8,128)S(1)}, f32[9,56,128]{...) custom-call(f32[384,128]{1,0:T(8,128)} %bitcast.9, ...), custom_call_target="tpu_custom_call" | custom-call | tf_op jit(solution)/shard_map/pallas_call | solution.py:601
  37.3 2.3 %shard_map.103 = (f32[384,128]{1,0:T(8,128)}, f32[384,128]{1,0:T(8,128)}, f32[384,128]{1,0:T(8,128)}, f32[384,128]{1,0:T(8,128)}) custom-call(f32[512,128]{1,0:T(8,128)S(1)} %get-tuple-element.16.p1, f32[512,128]{1,0:T(8,128)S(1)} %get-tuple-element.17.w1, f32[512,128]{1,0:T(8,128)S(1)} %get-tuple-element.18.u1, f32[512,128]{1,0:T(8,128)S(1)} %get-tuple-element.19.v1, ...), custom_call_target="tpu_custom_call" | custom-call | tf_op jit(solution)/shard_map/pallas_call | solution.py:633

commit v3 on v2

v3 whole, which is shorter than its diff:
```python
import functools

import jax
import jax.numpy as jnp
from jax import lax
from jax.experimental import pallas as pl
from jax.experimental.pallas import tpu as pltpu
from jax.sharding import PartitionSpec as P

MESH = pl.DeviceIdType.MESH
N = 48
H = 8
HALO = 14
SHIFT = 8
BASE = 3
ROWS = 56
FIRST = 40
REST = ROWS - FIRST
PART = 32
UP, DOWN = 7, 6
LINE = 8


def planes(ref, start, count):
    rows = pl.ds(pl.multiple_of(start * H, H), count * H)
    return ref[rows, :].reshape(count, H, 128)


def put(ref, start, value):
    rows = pl.ds(pl.multiple_of(start * H, H), value.shape[0] * H)
    ref[rows, :] = value.reshape(value.shape[0] * H, 128)


def row(ref, start, k):
    return ref[pl.ds(start * H + k, H, stride=H), :]


def put_row(ref, start, k, value):
    ref[pl.ds(start * H + k, H, stride=H), :] = value


def lat(value, steps):
    return pltpu.roll(value, steps % 128, 2)


def hgt(value, steps):
    return pltpu.roll(value, steps % H, 1)


def central(x, count):
    return 8.0 * (x[3 : 3 + count] - x[1 : 1 + count]) - (x[4 : 4 + count] - x[0:count])


def flows(src, dst, start, count, to, coef):
    press, vert, radial, lateral = src
    new_vert, new_radial, new_lateral = dst
    p = planes(press, start - 1, count + 3)
    u = planes(radial, start - 2, count + 4)
    v = planes(lateral, start - 2, count + 4)
    w = planes(vert, start - 2, count + 4)
    b1, a1, s0, s1, k0, k1, k2, km = (coef[i] for i in range(8))
    here, mid = p[1 : 1 + count], w[2 : 2 + count]
    put(
        new_radial,
        to,
        u[2 : 2 + count]
        - b1 * (27.0 * (p[2 : 2 + count] - here) - (p[3 : 3 + count] - p[0:count]))
        - a1 * central(u, count)
        - (s0 * mid + s1 * hgt(mid, 1)),
    )
    put(
        new_lateral,
        to,
        v[2 : 2 + count]
        - b1 * (27.0 * (lat(here, -1) - here) - (lat(here, -2) - lat(here, 1)))
        - a1 * central(v, count),
    )
    put(
        new_vert,
        to,
        mid
        + (k0 * here - k1 * hgt(here, -1))
        + (k2 * hgt(here, -2) - km * hgt(here, 1))
        - a1 * central(w, count),
    )


def pressures(press, new, dst, start, at, count, to, coef):
    new_vert, new_radial, new_lateral = new
    p = planes(press, start - 2, count + 4)
    u = planes(new_radial, at - 2, count + 3)
    v = planes(new_lateral, at, count)
    w = planes(new_vert, at, count)
    c1, a1, d1, d2, dm = coef[8], coef[1], coef[9], coef[10], coef[11]
    spread = (
        27.0 * (u[2 : 2 + count] - u[1 : 1 + count])
        - (u[3 : 3 + count] - u[0:count])
        + 27.0 * (v - lat(v, 1))
        - (lat(v, -1) - lat(v, 2))
        + (27.0 * w - d1 * hgt(w, 1))
        - (dm * hgt(w, -1) - d2 * hgt(w, 2))
    )
    put(dst, to, p[2 : 2 + count] - c1 * spread - a1 * central(p, count))


def line(ref, i):
    return jnp.broadcast_to(ref[pl.ds(i, 1), :], (H, 128))


def changes(coef, low_p, high_p, high_p2):
    b24 = coef.at[0]
    return (
        -line(b24, 0) * low_p,
        line(b24, 6) * high_p,
        line(b24, 7) * (high_p2 - 27.0 * high_p),
    )


def correct_pressure(ref, at, coef, du, d0, d6, d7, low1, low2, high):
    c24 = coef.at[8]
    for i, add in (
        (0, du + 27.0 * (d0 - low1) + low2),
        (1, low1 - 27.0 * d0),
        (2, d0),
        (5, -d6),
        (6, 27.0 * d6 - d7),
        (7, 27.0 * (d7 - d6) - high),
    ):
        put_row(ref, at, i, row(ref, at, i) - line(c24, i) * add)


def add_row(ref, at, i, value):
    new = row(ref, at, i) + value
    put_row(ref, at, i, new)
    return new


def both_steps(
    ranges,
    heights,
    press_in,
    vert_in,
    radial_in,
    lateral_in,
    stiff_in,
    buoy_in,
    wind_in,
    p2,
    w2,
    u2,
    v2,
    p0,
    w0,
    u0,
    v0,
    p1,
    w1,
    u1,
    v1,
    stiff,
    buoy,
    wind,
    up_send,
    up_recv,
    down_send,
    down_recv,
    low_w,
    halo,
    coef,
    low_more,
    high_more,
    local_sem,
    send_sem,
    recv_sem,
    ready,
):
    r, h = lax.axis_index("range"), lax.axis_index("height")
    first_r, last_r = r == 0, r == ranges - 1
    first_h, last_h = h == 0, h == heights - 1
    left = (lax.rem(r + ranges - 1, ranges), h)
    right = (lax.rem(r + 1, ranges), h)
    below = (r, lax.rem(h + heights - 1, heights))
    above = (r, lax.rem(h + 1, heights))
    no_left, no_right = jnp.logical_not(first_r), jnp.logical_not(last_r)
    no_below, no_above = jnp.logical_not(first_h), jnp.logical_not(last_h)
    odd = lax.rem(h, 2) == 1
    is_late = lax.rem(h // 2, 2) == 1
    is_early = jnp.logical_not(is_late)
    even = jnp.logical_not(odd)
    far_up, far_down = jnp.logical_and(odd, no_above), jnp.logical_and(even, no_below)
    near_up, near_down = jnp.logical_and(even, no_above), jnp.logical_and(odd, no_below)

    barrier = pltpu.get_barrier_semaphore()
    for there, device in (
        (no_right, right),
        (near_up, above),
        (near_down, below),
        (jnp.logical_and(is_early, far_up), above),
        (jnp.logical_and(is_early, far_down), below),
    ):

        @pl.when(there)
        def _():
            pl.semaphore_signal(barrier, inc=1, device_id=device, device_id_type=MESH)

    whole = pl.ds(0, N * H)
    loads = [
        pltpu.make_async_copy(src, dst, local_sem.at[i])
        for i, (src, dst) in enumerate(
            (
                (buoy_in, buoy),
                (stiff_in, stiff),
                (wind_in, wind),
                (press_in, p0.at[whole]),
                (vert_in, w0.at[whole]),
                (radial_in, u0.at[whole]),
                (lateral_in, v0.at[whole]),
            )
        )
    ]
    for load in loads:
        load.start()
    def remote(src, dst, i, device):
        return pltpu.make_async_remote_copy(
            src_ref=src,
            dst_ref=dst,
            send_sem=send_sem.at[i],
            recv_sem=recv_sem.at[i],
            device_id=device,
            device_id_type=MESH,
        )

    head, tail = pl.ds(0, HALO * H), pl.ds(N * H, HALO * H)
    ups = [remote(up_send[i], up_recv[i], i, above) for i in range(3)]
    downs = [remote(down_send[i], down_recv[i], 3 + i, below) for i in range(3)]
    lefts = [
        remote(src.at[head], dst.at[tail], 6 + i, left)
        for i, (src, dst) in enumerate(
            ((press_in, p0), (radial_in, u0), (vert_in, w0), (lateral_in, v0))
        )
    ]

    late_far = jnp.logical_and(is_late, jnp.logical_or(far_up, far_down))
    early_far = jnp.logical_and(is_early, jnp.logical_or(far_up, far_down))
    peers = sum(
        there.astype(jnp.int32)
        for there in (no_left, jnp.logical_or(near_up, near_down), late_far)
    )
    place = lax.rem(r, LINE)
    waits_long = jnp.logical_and(is_early, place == 0)

    def greet():
        pl.semaphore_wait(barrier, peers)
        for there, device in ((far_up, above), (far_down, below)):

            @pl.when(jnp.logical_and(is_late, there))
            def _():
                pl.semaphore_signal(ready, inc=1, device_id=device, device_id_type=MESH)

        @pl.when(no_left)
        def _():
            for copy in lefts:
                copy.start()

    pl.when(jnp.logical_not(waits_long))(greet)

    for load in loads[:3]:
        load.wait()

    k = lax.broadcasted_iota(jnp.int32, (H, 128), 0)
    lane = lax.broadcasted_iota(jnp.int32, (H, 128), 1)
    spread_wind = jnp.broadcast_to(wind[...], (H, 128))
    top = heights * H - 1

    def wind_at(rows):
        chosen = jnp.where(lane == rows, spread_wind, 0.0)
        return jnp.broadcast_to(jnp.sum(chosen, axis=1, keepdims=True), (H, 128))

    def shear_at(rows):
        upper = wind_at(jnp.where(rows < top, rows + 1, top))
        lower = wind_at(jnp.where(rows > 0, rows - 1, 0))
        return 0.5 * (upper - lower)

    mine = k + h * H
    b24, c24 = buoy[...] * (1.0 / 24.0), stiff[...] * (1.0 / 24.0)
    a12 = wind_at(mine) * (1.0 / 12.0)
    half_shear = 0.5 * shear_at(mine)
    b27 = b24 * 27.0
    full = jnp.full((H, 128), 27.0, jnp.float32)
    one = jnp.full((H, 128), 1.0, jnp.float32)
    for i, value in enumerate(
        (
            b24,
            a12,
            half_shear,
            jnp.where(k > 0, half_shear, 0.0),
            b27,
            jnp.where(k < H - 1, b27, 0.0),
            jnp.where(k < H - 2, b24, 0.0),
            jnp.where(k > 0, b24, 0.0),
            c24,
            jnp.where(k > 0, full, 0.0),
            jnp.where(k > 1, one, 0.0),
            jnp.where(k < H - 1, one, 0.0),
        )
    ):
        coef[i] = value
    for i, outside in enumerate((-1, -2, H)):
        coef[12 + i] = wind_at(jnp.zeros_like(k) + (h * H + outside)) * (1.0 / 12.0)
    s_low = 0.5 * shear_at(jnp.zeros_like(k) + h * H)
    s_high = 0.5 * shear_at(jnp.zeros_like(k) + (h * H + H))

    def free_flows(start, step, times):
        def body(j, carry):
            at = start + step * j
            flows((p0, w0, u0, v0), (w1, u1, v1), at, step, at, coef)
            return carry

        lax.fori_loop(0, times, body, 0)

    def free_pressures(start, step, times):
        def body(j, carry):
            at = start + step * j
            pressures(p0, (w1, u1, v1), p1, at, at, step, at, coef)
            return carry

        lax.fori_loop(0, times, body, 0)

    up_rows = ((p0, 7), (w0, 7)), ((w1, 7), (w1, 6)), ((p1, 7), (p1, 6), (p1, 5))
    down_rows = ((p0, 0), (p0, 1)), ((w1, 0),), ((p1, 0), (p1, 1), (p1, 2))

    def pack(buffer, to, rows, start, count):
        def body(j, carry):
            for q, (ref, height) in enumerate(rows):
                at = pl.ds(pl.multiple_of(to + q * count + j * H, H), H)
                buffer[at, :] = row(ref, start + H * j, height)
            return carry

        lax.fori_loop(0, count // H, body, 0)

    sides = (up_send, up_rows), (down_send, down_rows)

    def send(i):
        for there, copies in ((far_up, ups), (far_down, downs)):
            pl.when(jnp.logical_and(is_late, there))(copies[i].start)
        for there, copies in ((near_up, ups), (near_down, downs)):
            pl.when(there)(copies[i].start)

    for load in loads[3:]:
        load.wait()
    for buffers, (given, _, _) in sides:
        pack(buffers[0], 0, given, BASE, FIRST)
    next_w = line(w0, (BASE + FIRST) * H + 7)
    for_above = jnp.where(k == 3, next_w, jnp.where(k > 3, c24, pltpu.roll(b24, 2, 0)))
    up_send[0][pl.ds(2 * FIRST, H), :] = for_above
    down_send[0][pl.ds(2 * FIRST, H), :] = jnp.where(k < 4, c24, pltpu.roll(b24, 7, 0))
    pl.when(jnp.logical_not(waits_long))(lambda: send(0))
    free_flows(BASE, 6, 7)
    free_pressures(BASE, 5, 8)
    for buffers, (_, flow_rows, press_rows) in sides:
        pack(buffers[1], 0, flow_rows, BASE, FIRST)
        pack(buffers[1], len(flow_rows) * FIRST, press_rows, SHIFT, PART)

    @pl.when(waits_long)
    def _():
        greet()
        send(0)

    send(1)

    nothing = jnp.zeros((HALO * H, 128), jnp.float32)

    @pl.when(last_r)
    def _():
        for ref in (p0, u0, w0, v0):
            ref[tail, :] = nothing

    @pl.when(no_right)
    def _():
        for copy in lefts:
            copy.wait_recv()

    free_flows(45, 5, 3)

    def clear_after():
        for ref in (u1, v1, w1, p1):
            ref[pl.ds(N * H, 12 * H), :] = jnp.zeros((12 * H, 128), jnp.float32)

    pl.when(last_r)(clear_after)
    free_pressures(43, 4, 4)
    pl.when(last_r)(clear_after)
    for buffers, (given, flow_rows, press_rows) in sides:
        pack(buffers[2], 0, given + flow_rows, BASE + FIRST, REST)
        pack(buffers[2], len(given + flow_rows) * REST, press_rows, SHIFT + PART, REST)
    up_send[2][pl.ds(UP * REST, H), :] = row(w0, BASE + ROWS - H + 1, 7)
    send(2)

    for there, outgoing in ((far_up, ups), (far_down, downs)):

        @pl.when(jnp.logical_and(there, is_early))
        def _():
            pl.semaphore_wait(ready, 1)
            for copy in outgoing:
                copy.start()

    first_plane = jnp.where(first_r, SHIFT, 0)
    after_plane = jnp.where(last_r, N, 2 * N)

    def zero(ref, start, count):
        ref[pl.ds(start, count), :] = jnp.zeros((count, 128), jnp.float32)

    def arrived(parts):
        for none, some, copies, buffers in (
            (first_h, no_below, ups, up_recv),
            (last_h, no_above, downs, down_recv),
        ):

            @pl.when(some)
            def _():
                for i in parts:
                    copies[i].wait_recv()

            @pl.when(none)
            def _():
                for i in parts:
                    zero(buffers[i], 0, buffers[i].shape[0])

    def tile(ref, at):
        return ref[pl.ds(pl.multiple_of(at, H), H), :]

    def first_part(buffers, q, j):
        ref, at = (buffers[0], q) if q < 2 else (buffers[1], q - 2)
        return tile(ref, at * FIRST + j * H)

    def last_part(buffers, q, j):
        return tile(buffers[2], q * REST - FIRST + j * H)

    def first_pressure(buffers, flow_rows, q, j):
        return tile(buffers[1], flow_rows * FIRST + q * PART + j * H)

    def last_pressure(buffers, flow_rows, q, j):
        return tile(buffers[2], (2 + flow_rows + q) * REST - PART + j * H)

    def own_parts(at):
        own_p0, own_p1, own_p7 = row(p0, at, 0), row(p0, at, 1), row(p0, at, 7)
        return (
            line(low_more, 1) * (own_p1 - 27.0 * own_p0),
            line(low_more, 0) * own_p0,
            -line(high_more, 7) * own_p7,
        )

    def correct_first(part, j, carry):
        at = BASE + H * j
        here = pl.ds(pl.multiple_of(j * H, H), H)
        low_p0, _, low_w1, low_w2 = (part(up_recv, q, j) for q in range(4))
        high_p0, high_p1, high_w = (part(down_recv, q, j) for q in range(3))
        wl = [low_w[pl.ds(j * H + H + s, H), :] for s in (-2, -1, 0, 1)]
        e1, e2, e8 = own_parts(at)
        low_w1, low_w2, high_w = low_w1 + e1, low_w2 + e2, high_w + e8
        d0, d6, d7 = changes(coef, low_p0, high_p0, high_p1)
        for i, d in ((0, d0), (6, d6), (7, d7)):
            add_row(w1, at, i, d)
        add_row(u1, at, 0, -s_low * wl[2])
        du = -s_low * (27.0 * (wl[2] - wl[1]) - (wl[3] - wl[0]))
        correct_pressure(p1, at, coef, du, d0, d6, d7, low_w1, low_w2, high_w)
        plane = k + at
        keep = jnp.logical_and(plane >= first_plane, plane < after_plane)
        for i, value in enumerate((low_w1, low_w2, high_w)):
            halo[i, here, :] = jnp.where(keep, value, 0.0)
        return carry

    def second_flows(start, step, times):
        def body(j, carry):
            at = start + step * j
            flows((p1, w1, u1, v1), (w2, u2, v2), at + SHIFT, step, at + 2, coef)
            return carry

        lax.fori_loop(0, times, body, 0)

    def second_pressures(start, step, times):
        def body(j, carry):
            at = start + step * j
            pressures(p1, (w2, u2, v2), p2, at + SHIFT, at + 2, step, at, coef)
            return carry

        lax.fori_loop(0, times, body, 0)

    def correct_second(part, j, carry):
        at = H * j
        plane = at + SHIFT
        off = plane - BASE

        def rows_of(i, s=0):
            return halo[i, pl.ds(off + s, H), :]

        def across(i):
            return 8.0 * (rows_of(i, 1) - rows_of(i, -1)) - (rows_of(i, 2) - rows_of(i, -2))

        low_w1, low_w2, high_w = (rows_of(i) for i in range(3))
        e1, e2, e8 = own_parts(plane)
        new0, new6, new7 = (row(w1, plane, i) for i in (0, 6, 7))
        wt = [row(w0, plane + s, 7) for s in (-2, -1, 0, 1)]
        du_high = -s_high * (27.0 * (wt[2] - wt[1]) - (wt[3] - wt[0]))
        inside = k + plane < after_plane
        low_p1, low_p2, low_p3, high_p1, high_p2, high_p3 = (
            jnp.where(inside, value, 0.0)
            for value in (
                part(up_recv, 2, 0, j) - line(low_more, 7) * (27.0 * (e1 - e2) - new0),
                part(up_recv, 2, 1, j) - line(low_more, 6) * (27.0 * e2 - e1),
                part(up_recv, 2, 2, j) + line(low_more, 5) * e2,
                part(down_recv, 1, 0, j)
                - line(high_more, 0) * (du_high + 27.0 * (e8 - new7) + new6),
                part(down_recv, 1, 1, j) - line(high_more, 1) * (new7 - 27.0 * e8),
                part(down_recv, 1, 2, j) - line(high_more, 2) * e8,
            )
        )
        own_p0, own_p1, own_p7 = (row(p1, plane, i) for i in (0, 1, 7))
        d0, d6, d7 = changes(coef, low_p1, high_p1, high_p2)
        for i, d in ((0, d0), (6, d6), (7, d7)):
            add_row(w2, at + 2, i, d)
        du = -s_low * (27.0 * (low_w1 - rows_of(0, -1)) - (rows_of(0, 1) - rows_of(0, -2)))
        new1 = (
            low_w1
            - line(low_more, 1) * (27.0 * (own_p0 - low_p1) - (own_p1 - low_p2))
            - coef[12] * across(0)
        )
        new2 = (
            low_w2
            - line(low_more, 0) * (27.0 * (low_p1 - low_p2) - (own_p0 - low_p3))
            - coef[13] * across(1)
        )
        new8 = (
            high_w
            - line(high_more, 7) * (27.0 * (high_p2 - high_p1) - (high_p3 - own_p7))
            - coef[14] * across(2)
        )
        correct_pressure(p2, at, coef, du, d0, d6, d7, new1, new2, new8)
        return carry

    arrived((0, 1))
    more = pl.ds(2 * FIRST, H)
    low_more[...], high_more[...] = up_recv[0][more, :], down_recv[0][more, :]
    zero(low_w, 0, H)
    low_w[pl.ds(H, FIRST), :] = up_recv[0][pl.ds(FIRST, FIRST), :]
    low_w[pl.ds(H + FIRST, H), :] = line(low_more, 3)
    lax.fori_loop(0, FIRST // H, functools.partial(correct_first, first_part), 0)

    @pl.when(first_r)
    def _():
        for ref in (u1, v1, w1, p1):
            zero(ref, 0, SHIFT * H)

    second_flows(-2, 5, 7)
    pl.when(first_r)(lambda: zero(u2, 0, 2 * H))
    second_pressures(0, 8, PART // 8)
    lax.fori_loop(0, PART // H, functools.partial(correct_second, first_pressure), 0)

    arrived((2,))
    low_w[pl.ds(H + FIRST, REST), :] = up_recv[2][pl.ds(REST, REST), :]
    low_w[pl.ds(H + ROWS, H), :] = line(up_recv[2], UP * REST + H - 1)
    lax.fori_loop(FIRST // H, ROWS // H, functools.partial(correct_first, last_part), 0)
    pl.when(last_r)(clear_after)
    second_flows(PART + 1, 8, 2)
    second_pressures(PART, 8, (N - PART) // 8)
    lax.fori_loop(PART // H, N // H, functools.partial(correct_second, last_pressure), 0)

    def correct_radial(j, carry):
        rows = halo[0, pl.ds(H * j + SHIFT - BASE, H), :]
        add_row(u2, H * j + 2, 0, -s_low * rows)
        return carry

    lax.fori_loop(0, N // H, correct_radial, 0)

    @pl.when(no_above)
    def _():
        for copy in ups:
            copy.wait_send()

    @pl.when(no_below)
    def _():
        for copy in downs:
            copy.wait_send()

    @pl.when(no_left)
    def _():
        for copy in lefts:
            copy.wait_send()


def store(p2, w2, u2, v2, press_out, vert_out, radial_out, lateral_out, sems):
    inner = pl.ds(2 * H, N * H)
    copies = [
        pltpu.make_async_copy(src, dst, sems.at[i])
        for i, (src, dst) in enumerate(
            (
                (p2, press_out),
                (w2.at[inner], vert_out),
                (u2.at[inner], radial_out),
                (v2.at[inner], lateral_out),
            )
        )
    ]
    for copy in copies:
        copy.start()
    for copy in copies:
        copy.wait()


def solution(mesh):
    ranges, heights = mesh.shape["range"], mesh.shape["height"]

    def on_device(press, vert, radial, lateral, stiff, buoy, wind):
        def field(count):
            return pltpu.VMEM((count * H, 128), jnp.float32)

        def messages(rows, press_rows, more):
            flow_rows = rows - 2 - press_rows
            first = 2 * FIRST + H
            second = flow_rows * FIRST + press_rows * PART
            third = rows * REST + more * H
            return [pltpu.VMEM((count, 128), jnp.float32) for count in (first, second, third)]

        flat = [x.reshape(N * H, 128) for x in (press, vert, radial, lateral)]
        arguments = [
            pltpu.with_memory_space_constraint(x, pltpu.HBM)
            for x in (*flat, stiff, buoy, wind.reshape(1, 128))
        ]
        result = [field(N), field(N + 4), field(N + 4), field(N + 4)]
        state = pl.pallas_call(
            lambda *refs: both_steps(ranges, heights, *refs),
            out_shape=result,
            in_specs=[pl.BlockSpec(memory_space=pltpu.HBM)] * 7,
            out_specs=[pl.BlockSpec(memory_space=pltpu.VMEM)] * 4,
            scratch_shapes=[field(64)] * 8
            + [
                field(1),
                field(1),
                pltpu.VMEM((1, 128), jnp.float32),
                messages(UP, 3, 1),
                messages(UP, 3, 1),
                messages(DOWN, 3, 0),
                messages(DOWN, 3, 0),
                pltpu.VMEM((ROWS + 2 * H, 128), jnp.float32),
                pltpu.VMEM((3, ROWS, 128), jnp.float32),
                pltpu.VMEM((16, H, 128), jnp.float32),
                field(1),
                field(1),
                pltpu.SemaphoreType.DMA((7,)),
                pltpu.SemaphoreType.DMA((10,)),
                pltpu.SemaphoreType.DMA((10,)),
                pltpu.SemaphoreType.REGULAR,
            ],
            compiler_params=pltpu.CompilerParams(
                collective_id=0, has_side_effects=True, vmem_limit_bytes=24 * 2**20
            ),
        )(*arguments)
        out = pl.pallas_call(
            store,
            out_shape=[jax.ShapeDtypeStruct((N * H, 128), jnp.float32)] * 4,
            in_specs=[pl.BlockSpec(memory_space=pltpu.VMEM)] * 4,
            out_specs=[pl.BlockSpec(memory_space=pltpu.HBM)] * 4,
            scratch_shapes=[pltpu.SemaphoreType.DMA((4,))],
            compiler_params=pltpu.CompilerParams(vmem_limit_bytes=24 * 2**20),
        )(*state)
        return tuple(x.reshape(N, H, 128) for x in out)

    field_spec = P("range", "height", None)
    return jax.shard_map(
        on_device,
        mesh=mesh,
        in_specs=(field_spec,) * 4 + (P("height", None), P("height", None), P()),
        out_specs=(field_spec,) * 4,
        check_vma=False,
    )
```

time: 39.8 us -> 37.7 us (0.947)
  the two profiles are of different devices: /device:TPU:463 before, /device:TPU:471 now
where the time goes in v3:
time: 37.7 us; the launch traced here: 37.6 us
  Pallas kernels  36.9 us (98%)
  between operations  0.64 us (2%)
    pallas_call x1, Pallas kernels, on_device(): pl.pallas_call(lambda *refs: both_steps(ranges, heights, *refs), out_shap...  36 us
    pallas_call x1, Pallas kernels, on_device(): pl.pallas_call(store, out_shape=[jax.ShapeDtypeStruct((N * H, 128), jnp.f...  0.91 us

profile of v3, /device:TPU:471, one launch (start us, length us, event | category | flops | bytes accessed | tf_op | source)
XLA Modules:
  0.0 37.6 jit_solution(11837709571203049605)
XLA Ops:
  0.6 36.0 %shard_map.102 = (f32[384,128]{1,0:T(8,128)S(1)}, f32[416,128]{1,0:T(8,128)S(1)}, f32[416,128]{1,0:T(8,128)S(1)}, f32[416,128]{1,0:T(8,128)S(1)}) custom-call(f32[384,128]{1,0:T(8,128)} %bitcast.9, f32[384,128]{1,0:T(8,128)} %bitcast.10, f32[384,128]{1,0:T(8,128)} %bitcast.11, f32[384,128]{1,0:T(8,128)} %bitcast.12, f32[8,128]{1,0:T(8,128)} %refs_4_.1, ...), custom_call_target="tpu_custom_call" | custom-call | tf_op jit(solution)/shard_map/pallas_call | solution.py:629
  36.6 0.9 %shard_map.103 = (f32[384,128]{1,0:T(8,128)}, f32[384,128]{1,0:T(8,128)}, f32[384,128]{1,0:T(8,128)}, f32[384,128]{1,0:T(8,128)}) custom-call(f32[384,128]{1,0:T(8,128)S(1)} %get-tuple-element.12.p2, f32[416,128]{1,0:T(8,128)S(1)} %get-tuple-element.13.w2, f32[416,128]{1,0:T(8,128)S(1)} %get-tuple-element.14.u2, f32[416,128]{1,0:T(8,128)S(1)} %get-tuple-element.15.v2), custom_call_target="tpu_custom_call" | custom-call | tf_op jit(solution)/shard_map/pallas_call | solution.py:657

commit v4 on v3

--- a/solution.py
+++ b/solution.py
@@ -164,6 +164,8 @@
     up_recv,
     down_send,
     down_recv,
+    up_relay,
+    down_relay,
     low_w,
     halo,
     coef,
@@ -173,6 +175,7 @@
     send_sem,
     recv_sem,
     ready,
+    via_ready,
 ):
     r, h = lax.axis_index("range"), lax.axis_index("height")
     first_r, last_r = r == 0, r == ranges - 1
@@ -190,6 +193,14 @@
     far_up, far_down = jnp.logical_and(odd, no_above), jnp.logical_and(even, no_below)
     near_up, near_down = jnp.logical_and(even, no_above), jnp.logical_and(odd, no_below)
 
+    place = lax.rem(r, LINE)
+    has_far = jnp.logical_or(far_up, far_down)
+    goes_via = is_early & has_far & no_left & (place == LINE - 2)
+    ends_via = is_late & has_far & no_left & (place == LINE - 2)
+    relays = is_early & has_far & no_right & (place == LINE - 3)
+    left_above, left_below = (left[0], above[1]), (left[0], below[1])
+    right_above, right_below = (right[0], above[1]), (right[0], below[1])
+
     barrier = pltpu.get_barrier_semaphore()
     for there, device in (
         (no_right, right),
@@ -197,6 +208,8 @@
         (near_down, below),
         (jnp.logical_and(is_early, far_up), above),
         (jnp.logical_and(is_early, far_down), below),
+        (relays & far_up, right_above),
+        (relays & far_down, right_below),
     ):
 
         @pl.when(there)
@@ -220,11 +233,11 @@
     ]
     for load in loads:
         load.start()
-    def remote(src, dst, i, device):
+    def remote(src, dst, i, device, sending=None):
         return pltpu.make_async_remote_copy(
             src_ref=src,
             dst_ref=dst,
-            send_sem=send_sem.at[i],
+            send_sem=send_sem.at[i if sending is None else sending],
             recv_sem=recv_sem.at[i],
             device_id=device,
             device_id_type=MESH,
@@ -233,6 +246,14 @@
     head, tail = pl.ds(0, HALO * H), pl.ds(N * H, HALO * H)
     ups = [remote(up_send[i], up_recv[i], i, above) for i in range(3)]
     downs = [remote(down_send[i], down_recv[i], 3 + i, below) for i in range(3)]
+    vias = (
+        (far_up, remote(up_send[1], up_relay, 10, left)),
+        (far_down, remote(down_send[1], down_relay, 10, left)),
+    )
+    forwards = (
+        (far_up, remote(up_relay, up_recv[1], 1, right_above, 11)),
+        (far_down, remote(down_relay, down_recv[1], 4, right_below, 11)),
+    )
     lefts = [
         remote(src.at[head], dst.at[tail], 6 + i, left)
         for i, (src, dst) in enumerate(
@@ -244,18 +265,27 @@
     early_far = jnp.logical_and(is_early, jnp.logical_or(far_up, far_down))
     peers = sum(
         there.astype(jnp.int32)
-        for there in (no_left, jnp.logical_or(near_up, near_down), late_far)
-    )
-    place = lax.rem(r, LINE)
+        for there in (
+            no_left,
+            jnp.logical_or(near_up, near_down),
+            late_far,
+            ends_via,
+        )
+    )
     waits_long = jnp.logical_and(is_early, place == 0)
 
     def greet():
         pl.semaphore_wait(barrier, peers)
-        for there, device in ((far_up, above), (far_down, below)):
-
-            @pl.when(jnp.logical_and(is_late, there))
+        for there, device, signal in (
+            (is_late & far_up, above, ready),
+            (is_late & far_down, below, ready),
+            (ends_via & far_up, left_above, via_ready),
+            (ends_via & far_down, left_below, via_ready),
+        ):
+
+            @pl.when(there)
             def _():
-                pl.semaphore_signal(ready, inc=1, device_id=device, device_id_type=MESH)
+                pl.semaphore_signal(signal, inc=1, device_id=device, device_id_type=MESH)
 
         @pl.when(no_left)
         def _():
@@ -342,7 +372,10 @@
 
     def send(i):
         for there, copies in ((far_up, ups), (far_down, downs)):
-            pl.when(jnp.logical_and(is_late, there))(copies[i].start)
+            pl.when(is_late & there)(copies[i].start)
+        if i == 1:
+            for there, copy in vias:
+                pl.when(there & goes_via)(copy.start)
         for there, copies in ((near_up, ups), (near_down, downs)):
             pl.when(there)(copies[i].start)
 
@@ -368,6 +401,15 @@
 
     send(1)
 
+    eager = jnp.logical_and(is_early, place == LINE - 1)
+    for there, outgoing in ((far_up, ups), (far_down, downs)):
+
+        @pl.when(jnp.logical_and(there, eager))
+        def _():
+            pl.semaphore_wait(ready, 1)
+            for copy in outgoing[:2]:
+                copy.start()
+
     nothing = jnp.zeros((HALO * H, 128), jnp.float32)
 
     @pl.when(last_r)
@@ -396,12 +438,22 @@
     send(2)
 
     for there, outgoing in ((far_up, ups), (far_down, downs)):
-
-        @pl.when(jnp.logical_and(there, is_early))
+        pl.when(jnp.logical_and(there, eager))(outgoing[2].start)
+
+        @pl.when(jnp.logical_and(there, jnp.logical_and(is_early, jnp.logical_not(eager))))
         def _():
             pl.semaphore_wait(ready, 1)
-            for copy in outgoing:
-                copy.start()
+            outgoing[0].start()
+            pl.when(jnp.logical_not(goes_via))(outgoing[1].start)
+            outgoing[2].start()
+
+    pl.when(relays)(lambda: pl.semaphore_wait(via_ready, 1))
+    for (there, came), (_, copy) in zip(vias, forwards):
+
+        @pl.when(there & relays)
+        def _():
+            came.wait_recv()
+            copy.start()
 
     first_plane = jnp.where(first_r, SHIFT, 0)
     after_plane = jnp.where(last_r, N, 2 * N)
@@ -571,15 +623,18 @@
 
     lax.fori_loop(0, N // H, correct_radial, 0)
 
-    @pl.when(no_above)
-    def _():
-        for copy in ups:
-            copy.wait_send()
-
-    @pl.when(no_below)
-    def _():
-        for copy in downs:
-            copy.wait_send()
+    for some, far, copies in ((no_above, far_up, ups), (no_below, far_down, downs)):
+
+        @pl.when(some)
+        def _():
+            copies[0].wait_send()
+            pl.when(jnp.logical_not(far & goes_via))(copies[1].wait_send)
+            copies[2].wait_send()
+
+    for there, copy in vias:
+        pl.when(there & goes_via)(copy.wait_send)
+    for there, copy in forwards:
+        pl.when(there & relays)(copy.wait_send)
 
     @pl.when(no_left)
     def _():
@@ -640,14 +695,17 @@
                 messages(UP, 3, 1),
                 messages(DOWN, 3, 0),
                 messages(DOWN, 3, 0),
+                messages(UP, 3, 1)[1],
+                messages(DOWN, 3, 0)[1],
                 pltpu.VMEM((ROWS + 2 * H, 128), jnp.float32),
                 pltpu.VMEM((3, ROWS, 128), jnp.float32),
                 pltpu.VMEM((16, H, 128), jnp.float32),
                 field(1),
                 field(1),
                 pltpu.SemaphoreType.DMA((7,)),
-                pltpu.SemaphoreType.DMA((10,)),
-                pltpu.SemaphoreType.DMA((10,)),
+                pltpu.SemaphoreType.DMA((12,)),
+                pltpu.SemaphoreType.DMA((11,)),
+                pltpu.SemaphoreType.REGULAR,
                 pltpu.SemaphoreType.REGULAR,
             ],
             compiler_params=pltpu.CompilerParams(

time: 37.7 us -> 36.4 us (0.966)
  the two profiles are of different devices: /device:TPU:471 before, /device:TPU:463 now
where the time goes in v4:
time: 36.4 us; the launch traced here: 36.2 us
  Pallas kernels  35.6 us (98%)
  between operations  0.64 us (2%)
    pallas_call x1, Pallas kernels, on_device(): pl.pallas_call(lambda *refs: both_steps(ranges, heights, *refs), out_shap...  34.7 us
    pallas_call x1, Pallas kernels, on_device(): pl.pallas_call(store, out_shape=[jax.ShapeDtypeStruct((N * H, 128), jnp.f...  0.91 us

profile of v4, /device:TPU:463, one launch (start us, length us, event | category | flops | bytes accessed | tf_op | source)
XLA Modules:
  0.0 36.2 jit_solution(17899604093495991666)
XLA Ops:
  0.6 34.7 %shard_map.102 = (f32[384,128]{1,0:T(8,128)S(1)}, f32[416,128]{1,0:T(8,128)S(1)}, f32[416,128]{1,0:T(8,128)S(1)}, f32[416,128]{1,0:T(8,128)S(1)}) custom-call(f32[384,128]{1,0:T(8,128)} %bitcast.9, f32[384,128]{1,0:T(8,128)} %bitcast.10, f32[384,128]{1,0:T(8,128)} %bitcast.11, f32[384,128]{1,0:T(8,128)} %bitcast.12, f32[8,128]{1,0:T(8,128)} %refs_4_.1, ...), custom_call_target="tpu_custom_call" | custom-call | tf_op jit(solution)/shard_map/pallas_call | solution.py:684
  35.3 0.9 %shard_map.103 = (f32[384,128]{1,0:T(8,128)}, f32[384,128]{1,0:T(8,128)}, f32[384,128]{1,0:T(8,128)}, f32[384,128]{1,0:T(8,128)}) custom-call(f32[384,128]{1,0:T(8,128)S(1)} %get-tuple-element.12.p2, f32[416,128]{1,0:T(8,128)S(1)} %get-tuple-element.13.w2, f32[416,128]{1,0:T(8,128)S(1)} %get-tuple-element.14.u2, f32[416,128]{1,0:T(8,128)S(1)} %get-tuple-element.15.v2), custom_call_target="tpu_custom_call" | custom-call | tf_op jit(solution)/shard_map/pallas_call | solution.py:715

commit v5 on v4

--- a/solution.py
+++ b/solution.py
@@ -243,7 +243,7 @@
             device_id_type=MESH,
         )
 
-    head, tail = pl.ds(0, HALO * H), pl.ds(N * H, HALO * H)
+    tail = pl.ds(N * H, HALO * H)
     ups = [remote(up_send[i], up_recv[i], i, above) for i in range(3)]
     downs = [remote(down_send[i], down_recv[i], 3 + i, below) for i in range(3)]
     vias = (
@@ -255,9 +255,14 @@
         (far_down, remote(down_relay, down_recv[1], 4, right_below, 11)),
     )
     lefts = [
-        remote(src.at[head], dst.at[tail], 6 + i, left)
-        for i, (src, dst) in enumerate(
-            ((press_in, p0), (radial_in, u0), (vert_in, w0), (lateral_in, v0))
+        remote(src.at[pl.ds(0, count * H)], dst.at[pl.ds(N * H, count * H)], 6 + i, left)
+        for i, (src, dst, count) in enumerate(
+            (
+                (press_in, p0, HALO),
+                (radial_in, u0, HALO),
+                (vert_in, w0, HALO - 1),
+                (lateral_in, v0, HALO - 1),
+            )
         )
     ]
 
@@ -356,14 +361,22 @@
 
         lax.fori_loop(0, times, body, 0)
 
-    up_rows = ((p0, 7), (w0, 7)), ((w1, 7), (w1, 6)), ((p1, 7), (p1, 6), (p1, 5))
-    down_rows = ((p0, 0), (p0, 1)), ((w1, 0),), ((p1, 0), (p1, 1), (p1, 2))
+    up_rows = (
+        ((p0, 7, 0), (w0, 7, 1)),
+        ((w1, 7, 0), (w1, 6, 0)),
+        ((p1, 7, 0), (p1, 6, 0), (p1, 5, 0)),
+    )
+    down_rows = (
+        ((p0, 0, 0), (p0, 1, 0)),
+        ((w1, 0, 0),),
+        ((p1, 0, 0), (p1, 1, 0), (p1, 2, 0)),
+    )
 
     def pack(buffer, to, rows, start, count):
         def body(j, carry):
-            for q, (ref, height) in enumerate(rows):
+            for q, (ref, height, later) in enumerate(rows):
                 at = pl.ds(pl.multiple_of(to + q * count + j * H, H), H)
-                buffer[at, :] = row(ref, start + H * j, height)
+                buffer[at, :] = row(ref, start + later + H * j, height)
             return carry
 
         lax.fori_loop(0, count // H, body, 0)
@@ -383,8 +396,8 @@
         load.wait()
     for buffers, (given, _, _) in sides:
         pack(buffers[0], 0, given, BASE, FIRST)
-    next_w = line(w0, (BASE + FIRST) * H + 7)
-    for_above = jnp.where(k == 3, next_w, jnp.where(k > 3, c24, pltpu.roll(b24, 2, 0)))
+    first_w = line(w0, BASE * H + 7)
+    for_above = jnp.where(k == 3, first_w, jnp.where(k > 3, c24, pltpu.roll(b24, 2, 0)))
     up_send[0][pl.ds(2 * FIRST, H), :] = for_above
     down_send[0][pl.ds(2 * FIRST, H), :] = jnp.where(k < 4, c24, pltpu.roll(b24, 7, 0))
     pl.when(jnp.logical_not(waits_long))(lambda: send(0))
@@ -434,7 +447,6 @@
     for buffers, (given, flow_rows, press_rows) in sides:
         pack(buffers[2], 0, given + flow_rows, BASE + FIRST, REST)
         pack(buffers[2], len(given + flow_rows) * REST, press_rows, SHIFT + PART, REST)
-    up_send[2][pl.ds(UP * REST, H), :] = row(w0, BASE + ROWS - H + 1, 7)
     send(2)
 
     for there, outgoing in ((far_up, ups), (far_down, downs)):
@@ -593,8 +605,8 @@
     more = pl.ds(2 * FIRST, H)
     low_more[...], high_more[...] = up_recv[0][more, :], down_recv[0][more, :]
     zero(low_w, 0, H)
-    low_w[pl.ds(H, FIRST), :] = up_recv[0][pl.ds(FIRST, FIRST), :]
-    low_w[pl.ds(H + FIRST, H), :] = line(low_more, 3)
+    low_w[pl.ds(H, 1), :] = low_more[pl.ds(3, 1), :]
+    low_w[pl.ds(H + 1, FIRST), :] = up_recv[0][pl.ds(FIRST, FIRST), :]
     lax.fori_loop(0, FIRST // H, functools.partial(correct_first, first_part), 0)
 
     @pl.when(first_r)
@@ -608,8 +620,7 @@
     lax.fori_loop(0, PART // H, functools.partial(correct_second, first_pressure), 0)
 
     arrived((2,))
-    low_w[pl.ds(H + FIRST, REST), :] = up_recv[2][pl.ds(REST, REST), :]
-    low_w[pl.ds(H + ROWS, H), :] = line(up_recv[2], UP * REST + H - 1)
+    low_w[pl.ds(H + 1 + FIRST, REST), :] = up_recv[2][pl.ds(REST, REST), :]
     lax.fori_loop(FIRST // H, ROWS // H, functools.partial(correct_first, last_part), 0)
     pl.when(last_r)(clear_after)
     second_flows(PART + 1, 8, 2)
@@ -668,11 +679,11 @@
         def field(count):
             return pltpu.VMEM((count * H, 128), jnp.float32)
 
-        def messages(rows, press_rows, more):
+        def messages(rows, press_rows):
             flow_rows = rows - 2 - press_rows
             first = 2 * FIRST + H
             second = flow_rows * FIRST + press_rows * PART
-            third = rows * REST + more * H
+            third = rows * REST
             return [pltpu.VMEM((count, 128), jnp.float32) for count in (first, second, third)]
 
         flat = [x.reshape(N * H, 128) for x in (press, vert, radial, lateral)]
@@ -691,12 +702,12 @@
                 field(1),
                 field(1),
                 pltpu.VMEM((1, 128), jnp.float32),
-                messages(UP, 3, 1),
-                messages(UP, 3, 1),
-                messages(DOWN, 3, 0),
-                messages(DOWN, 3, 0),
-                messages(UP, 3, 1)[1],
-                messages(DOWN, 3, 0)[1],
+                messages(UP, 3),
+                messages(UP, 3),
+                messages(DOWN, 3),
+                messages(DOWN, 3),
+                messages(UP, 3)[1],
+                messages(DOWN, 3)[1],
                 pltpu.VMEM((ROWS + 2 * H, 128), jnp.float32),
                 pltpu.VMEM((3, ROWS, 128), jnp.float32),
                 pltpu.VMEM((16, H, 128), jnp.float32),

time: 36.4 us -> 36 us (0.989)
  no operation moved by 1% of the time
where the time goes in v5:
time: 36 us; the launch traced here: 35.9 us
  Pallas kernels  35.3 us (98%)
  between operations  0.64 us (2%)
    pallas_call x1, Pallas kernels, on_device(): pl.pallas_call(lambda *refs: both_steps(ranges, heights, *refs), out_shap...  34.3 us
    pallas_call x1, Pallas kernels, on_device(): pl.pallas_call(store, out_shape=[jax.ShapeDtypeStruct((N * H, 128), jnp.f...  0.91 us

profile of v5, /device:TPU:463, one launch (start us, length us, event | category | flops | bytes accessed | tf_op | source)
XLA Modules:
  0.0 35.9 jit_solution(15543425802923925410)
XLA Ops:
  0.6 34.3 %shard_map.102 = (f32[384,128]{1,0:T(8,128)S(1)}, f32[416,128]{1,0:T(8,128)S(1)}, f32[416,128]{1,0:T(8,128)S(1)}, f32[416,128]{1,0:T(8,128)S(1)}) custom-call(f32[384,128]{1,0:T(8,128)} %bitcast.9, f32[384,128]{1,0:T(8,128)} %bitcast.10, f32[384,128]{1,0:T(8,128)} %bitcast.11, f32[384,128]{1,0:T(8,128)} %bitcast.12, f32[8,128]{1,0:T(8,128)} %refs_4_.1, ...), custom_call_target="tpu_custom_call" | custom-call | tf_op jit(solution)/shard_map/pallas_call | solution.py:695
  35.0 0.9 %shard_map.103 = (f32[384,128]{1,0:T(8,128)}, f32[384,128]{1,0:T(8,128)}, f32[384,128]{1,0:T(8,128)}, f32[384,128]{1,0:T(8,128)}) custom-call(f32[384,128]{1,0:T(8,128)S(1)} %get-tuple-element.12.p2, f32[416,128]{1,0:T(8,128)S(1)} %get-tuple-element.13.w2, f32[416,128]{1,0:T(8,128)S(1)} %get-tuple-element.14.u2, f32[416,128]{1,0:T(8,128)S(1)} %get-tuple-element.15.v2), custom_call_target="tpu_custom_call" | custom-call | tf_op jit(solution)/shard_map/pallas_call | solution.py:726

commit v6 on v5

--- a/solution.py
+++ b/solution.py
@@ -1,4 +1,6 @@
 import functools
+from collections.abc import Callable
+from typing import NamedTuple
 
 import jax
 import jax.numpy as jnp
@@ -135,6 +137,173 @@
     return new
 
 
+def zero(ref, start, count):
+    ref[pl.ds(start, count), :] = jnp.zeros((count, 128), jnp.float32)
+
+
+class Finish(NamedTuple):
+    first: Callable
+    last: Callable
+    radial: Callable
+
+
+def finishing(
+    ranges, p0, w0, p1, w1, u1, v1, p2, w2, u2, v2, up_recv, down_recv, low_w, halo, coef, low_more, high_more
+):
+    r = lax.axis_index("range")
+    first_r, last_r = r == 0, r == ranges - 1
+    k = lax.broadcasted_iota(jnp.int32, (H, 128), 0)
+    first_plane = jnp.where(first_r, SHIFT, 0)
+    after_plane = jnp.where(last_r, N, 2 * N)
+    s_low, s_high = coef[15], coef[16]
+
+    def clear_after():
+        for ref in (u1, v1, w1, p1):
+            zero(ref, N * H, 12 * H)
+
+    def tile(ref, at):
+        return ref[pl.ds(pl.multiple_of(at, H), H), :]
+
+    def first_part(buffers, q, j):
+        ref, at = (buffers[0], q) if q < 2 else (buffers[1], q - 2)
+        return tile(ref, at * FIRST + j * H)
+
+    def last_part(buffers, q, j):
+        return tile(buffers[2], q * REST - FIRST + j * H)
+
+    def first_pressure(buffers, flow_rows, q, j):
+        return tile(buffers[1], flow_rows * FIRST + q * PART + j * H)
+
+    def last_pressure(buffers, flow_rows, q, j):
+        return tile(buffers[2], (2 + flow_rows + q) * REST - PART + j * H)
+
+    def own_parts(at):
+        own_p0, own_p1, own_p7 = row(p0, at, 0), row(p0, at, 1), row(p0, at, 7)
+        return (
+            line(low_more, 1) * (own_p1 - 27.0 * own_p0),
+            line(low_more, 0) * own_p0,
+            -line(high_more, 7) * own_p7,
+        )
+
+    def correct_first(part, j, carry):
+        at = BASE + H * j
+        here = pl.ds(pl.multiple_of(j * H, H), H)
+        low_p0, _, low_w1, low_w2 = (part(up_recv, q, j) for q in range(4))
+        high_p0, high_p1, high_w = (part(down_recv, q, j) for q in range(3))
+        wl = [low_w[pl.ds(j * H + H + s, H), :] for s in (-2, -1, 0, 1)]
+        e1, e2, e8 = own_parts(at)
+        low_w1, low_w2, high_w = low_w1 + e1, low_w2 + e2, high_w + e8
+        d0, d6, d7 = changes(coef, low_p0, high_p0, high_p1)
+        for i, d in ((0, d0), (6, d6), (7, d7)):
+            add_row(w1, at, i, d)
+        add_row(u1, at, 0, -s_low * wl[2])
+        du = -s_low * (27.0 * (wl[2] - wl[1]) - (wl[3] - wl[0]))
+        correct_pressure(p1, at, coef, du, d0, d6, d7, low_w1, low_w2, high_w)
+        plane = k + at
+        keep = jnp.logical_and(plane >= first_plane, plane < after_plane)
+        for i, value in enumerate((low_w1, low_w2, high_w)):
+            halo[i, here, :] = jnp.where(keep, value, 0.0)
+        return carry
+
+    def second_flows(start, step, times):
+        def body(j, carry):
+            at = start + step * j
+            flows((p1, w1, u1, v1), (w2, u2, v2), at + SHIFT, step, at + 2, coef)
+            return carry
+
+        lax.fori_loop(0, times, body, 0)
+
+    def second_pressures(start, step, times):
+        def body(j, carry):
+            at = start + step * j
+            pressures(p1, (w2, u2, v2), p2, at + SHIFT, at + 2, step, at, coef)
+            return carry
+
+        lax.fori_loop(0, times, body, 0)
+
+    def correct_second(part, j, carry):
+        at = H * j
+        plane = at + SHIFT
+        off = plane - BASE
+
+        def rows_of(i, s=0):
+            return halo[i, pl.ds(off + s, H), :]
+
+        def across(i):
+            return 8.0 * (rows_of(i, 1) - rows_of(i, -1)) - (rows_of(i, 2) - rows_of(i, -2))
+
+        low_w1, low_w2, high_w = (rows_of(i) for i in range(3))
+        e1, e2, e8 = own_parts(plane)
+        new0, new6, new7 = (row(w1, plane, i) for i in (0, 6, 7))
+        wt = [row(w0, plane + s, 7) for s in (-2, -1, 0, 1)]
+        du_high = -s_high * (27.0 * (wt[2] - wt[1]) - (wt[3] - wt[0]))
+        inside = k + plane < after_plane
+        low_p1, low_p2, low_p3, high_p1, high_p2, high_p3 = (
+            jnp.where(inside, value, 0.0)
+            for value in (
+                part(up_recv, 2, 0, j) - line(low_more, 7) * (27.0 * (e1 - e2) - new0),
+                part(up_recv, 2, 1, j) - line(low_more, 6) * (27.0 * e2 - e1),
+                part(up_recv, 2, 2, j) + line(low_more, 5) * e2,
+                part(down_recv, 1, 0, j)
+                - line(high_more, 0) * (du_high + 27.0 * (e8 - new7) + new6),
+                part(down_recv, 1, 1, j) - line(high_more, 1) * (new7 - 27.0 * e8),
+                part(down_recv, 1, 2, j) - line(high_more, 2) * e8,
+            )
+        )
+        own_p0, own_p1, own_p7 = (row(p1, plane, i) for i in (0, 1, 7))
+        d0, d6, d7 = changes(coef, low_p1, high_p1, high_p2)
+        for i, d in ((0, d0), (6, d6), (7, d7)):
+            add_row(w2, at + 2, i, d)
+        du = -s_low * (27.0 * (low_w1 - rows_of(0, -1)) - (rows_of(0, 1) - rows_of(0, -2)))
+        new1 = (
+            low_w1
+            - line(low_more, 1) * (27.0 * (own_p0 - low_p1) - (own_p1 - low_p2))
+            - coef[12] * across(0)
+        )
+        new2 = (
+            low_w2
+            - line(low_more, 0) * (27.0 * (low_p1 - low_p2) - (own_p0 - low_p3))
+            - coef[13] * across(1)
+        )
+        new8 = (
+            high_w
+            - line(high_more, 7) * (27.0 * (high_p2 - high_p1) - (high_p3 - own_p7))
+            - coef[14] * across(2)
+        )
+        correct_pressure(p2, at, coef, du, d0, d6, d7, new1, new2, new8)
+        return carry
+
+    def first():
+        lax.fori_loop(0, FIRST // H, functools.partial(correct_first, first_part), 0)
+
+        @pl.when(first_r)
+        def _():
+            for ref in (u1, v1, w1, p1):
+                zero(ref, 0, SHIFT * H)
+
+        second_flows(-2, 5, 7)
+        pl.when(first_r)(lambda: zero(u2, 0, 2 * H))
+        second_pressures(0, 8, PART // 8)
+        lax.fori_loop(0, PART // H, functools.partial(correct_second, first_pressure), 0)
+
+    def last():
+        lax.fori_loop(FIRST // H, ROWS // H, functools.partial(correct_first, last_part), 0)
+        pl.when(last_r)(clear_after)
+        second_flows(PART + 1, 8, 2)
+        second_pressures(PART, 8, (N - PART) // 8)
+        lax.fori_loop(PART // H, N // H, functools.partial(correct_second, last_pressure), 0)
+
+    def correct_radial(j, carry):
+        rows = halo[0, pl.ds(H * j + SHIFT - BASE, H), :]
+        add_row(u2, H * j + 2, 0, -s_low * rows)
+        return carry
+
+    def radial(start, stop):
+        lax.fori_loop(start // H, stop // H, correct_radial, 0)
+
+    return Finish(first, last, radial)
+
+
 def both_steps(
     ranges,
     heights,
@@ -151,32 +320,35 @@
     v2,
     p0,
     w0,
-    u0,
-    v0,
     p1,
     w1,
     u1,
     v1,
-    stiff,
-    buoy,
-    wind,
-    up_send,
-    up_recv,
-    down_send,
-    down_recv,
-    up_relay,
-    down_relay,
+    up_last,
+    down_last,
     low_w,
     halo,
     coef,
     low_more,
     high_more,
+    u0,
+    v0,
+    stiff,
+    buoy,
+    wind,
+    up_send,
+    up_first,
+    down_send,
+    down_first,
+    up_relay,
+    down_relay,
     local_sem,
     send_sem,
     recv_sem,
     ready,
     via_ready,
 ):
+    up_recv, down_recv = [*up_first, up_last], [*down_first, down_last]
     r, h = lax.axis_index("range"), lax.axis_index("height")
     first_r, last_r = r == 0, r == ranges - 1
     first_h, last_h = h == 0, h == heights - 1
@@ -342,8 +514,8 @@
         coef[i] = value
     for i, outside in enumerate((-1, -2, H)):
         coef[12 + i] = wind_at(jnp.zeros_like(k) + (h * H + outside)) * (1.0 / 12.0)
-    s_low = 0.5 * shear_at(jnp.zeros_like(k) + h * H)
-    s_high = 0.5 * shear_at(jnp.zeros_like(k) + (h * H + H))
+    coef[15] = 0.5 * shear_at(jnp.zeros_like(k) + h * H)
+    coef[16] = 0.5 * shear_at(jnp.zeros_like(k) + (h * H + H))
 
     def free_flows(start, step, times):
         def body(j, carry):
@@ -467,12 +639,6 @@
             came.wait_recv()
             copy.start()
 
-    first_plane = jnp.where(first_r, SHIFT, 0)
-    after_plane = jnp.where(last_r, N, 2 * N)
-
-    def zero(ref, start, count):
-        ref[pl.ds(start, count), :] = jnp.zeros((count, 128), jnp.float32)
-
     def arrived(parts):
         for none, some, copies, buffers in (
             (first_h, no_below, ups, up_recv),
@@ -489,117 +655,9 @@
                 for i in parts:
                     zero(buffers[i], 0, buffers[i].shape[0])
 
-    def tile(ref, at):
-        return ref[pl.ds(pl.multiple_of(at, H), H), :]
-
-    def first_part(buffers, q, j):
-        ref, at = (buffers[0], q) if q < 2 else (buffers[1], q - 2)
-        return tile(ref, at * FIRST + j * H)
-
-    def last_part(buffers, q, j):
-        return tile(buffers[2], q * REST - FIRST + j * H)
-
-    def first_pressure(buffers, flow_rows, q, j):
-        return tile(buffers[1], flow_rows * FIRST + q * PART + j * H)
-
-    def last_pressure(buffers, flow_rows, q, j):
-        return tile(buffers[2], (2 + flow_rows + q) * REST - PART + j * H)
-
-    def own_parts(at):
-        own_p0, own_p1, own_p7 = row(p0, at, 0), row(p0, at, 1), row(p0, at, 7)
-        return (
-            line(low_more, 1) * (own_p1 - 27.0 * own_p0),
-            line(low_more, 0) * own_p0,
-            -line(high_more, 7) * own_p7,
-        )
-
-    def correct_first(part, j, carry):
-        at = BASE + H * j
-        here = pl.ds(pl.multiple_of(j * H, H), H)
-        low_p0, _, low_w1, low_w2 = (part(up_recv, q, j) for q in range(4))
-        high_p0, high_p1, high_w = (part(down_recv, q, j) for q in range(3))
-        wl = [low_w[pl.ds(j * H + H + s, H), :] for s in (-2, -1, 0, 1)]
-        e1, e2, e8 = own_parts(at)
-        low_w1, low_w2, high_w = low_w1 + e1, low_w2 + e2, high_w + e8
-        d0, d6, d7 = changes(coef, low_p0, high_p0, high_p1)
-        for i, d in ((0, d0), (6, d6), (7, d7)):
-            add_row(w1, at, i, d)
-        add_row(u1, at, 0, -s_low * wl[2])
-        du = -s_low * (27.0 * (wl[2] - wl[1]) - (wl[3] - wl[0]))
-        correct_pressure(p1, at, coef, du, d0, d6, d7, low_w1, low_w2, high_w)
-        plane = k + at
-        keep = jnp.logical_and(plane >= first_plane, plane < after_plane)
-        for i, value in enumerate((low_w1, low_w2, high_w)):
-            halo[i, here, :] = jnp.where(keep, value, 0.0)
-        return carry
-
-    def second_flows(start, step, times):
-        def body(j, carry):
-            at = start + step * j
-            flows((p1, w1, u1, v1), (w2, u2, v2), at + SHIFT, step, at + 2, coef)
-            return carry
-
-        lax.fori_loop(0, times, body, 0)
-
-    def second_pressures(start, step, times):
-        def body(j, carry):
-            at = start + step * j
-            pressures(p1, (w2, u2, v2), p2, at + SHIFT, at + 2, step, at, coef)
-            return carry
-
-        lax.fori_loop(0, times, body, 0)
-
-    def correct_second(part, j, carry):
-        at = H * j
-        plane = at + SHIFT
-        off = plane - BASE
-
-        def rows_of(i, s=0):
-            return halo[i, pl.ds(off + s, H), :]
-
-        def across(i):
-            return 8.0 * (rows_of(i, 1) - rows_of(i, -1)) - (rows_of(i, 2) - rows_of(i, -2))
-
-        low_w1, low_w2, high_w = (rows_of(i) for i in range(3))
-        e1, e2, e8 = own_parts(plane)
-        new0, new6, new7 = (row(w1, plane, i) for i in (0, 6, 7))
-        wt = [row(w0, plane + s, 7) for s in (-2, -1, 0, 1)]
-        du_high = -s_high * (27.0 * (wt[2] - wt[1]) - (wt[3] - wt[0]))
-        inside = k + plane < after_plane
-        low_p1, low_p2, low_p3, high_p1, high_p2, high_p3 = (
-            jnp.where(inside, value, 0.0)
-            for value in (
-                part(up_recv, 2, 0, j) - line(low_more, 7) * (27.0 * (e1 - e2) - new0),
-                part(up_recv, 2, 1, j) - line(low_more, 6) * (27.0 * e2 - e1),
-                part(up_recv, 2, 2, j) + line(low_more, 5) * e2,
-                part(down_recv, 1, 0, j)
-                - line(high_more, 0) * (du_high + 27.0 * (e8 - new7) + new6),
-                part(down_recv, 1, 1, j) - line(high_more, 1) * (new7 - 27.0 * e8),
-                part(down_recv, 1, 2, j) - line(high_more, 2) * e8,
-            )
-        )
-        own_p0, own_p1, own_p7 = (row(p1, plane, i) for i in (0, 1, 7))
-        d0, d6, d7 = changes(coef, low_p1, high_p1, high_p2)
-        for i, d in ((0, d0), (6, d6), (7, d7)):
-            add_row(w2, at + 2, i, d)
-        du = -s_low * (27.0 * (low_w1 - rows_of(0, -1)) - (rows_of(0, 1) - rows_of(0, -2)))
-        new1 = (
-            low_w1
-            - line(low_more, 1) * (27.0 * (own_p0 - low_p1) - (own_p1 - low_p2))
-            - coef[12] * across(0)
-        )
-        new2 = (
-            low_w2
-            - line(low_more, 0) * (27.0 * (low_p1 - low_p2) - (own_p0 - low_p3))
-            - coef[13] * across(1)
-        )
-        new8 = (
-            high_w
-            - line(high_more, 7) * (27.0 * (high_p2 - high_p1) - (high_p3 - own_p7))
-            - coef[14] * across(2)
-        )
-        correct_pressure(p2, at, coef, du, d0, d6, d7, new1, new2, new8)
-        return carry
+    finish = finishing(
+        ranges, p0, w0, p1, w1, u1, v1, p2, w2, u2, v2, up_recv, down_recv, low_w, halo, coef, low_more, high_more
+    )
 
     arrived((0, 1))
     more = pl.ds(2 * FIRST, H)
@@ -607,33 +665,10 @@
     zero(low_w, 0, H)
     low_w[pl.ds(H, 1), :] = low_more[pl.ds(3, 1), :]
     low_w[pl.ds(H + 1, FIRST), :] = up_recv[0][pl.ds(FIRST, FIRST), :]
-    lax.fori_loop(0, FIRST // H, functools.partial(correct_first, first_part), 0)
-
-    @pl.when(first_r)
-    def _():
-        for ref in (u1, v1, w1, p1):
-            zero(ref, 0, SHIFT * H)
-
-    second_flows(-2, 5, 7)
-    pl.when(first_r)(lambda: zero(u2, 0, 2 * H))
-    second_pressures(0, 8, PART // 8)
-    lax.fori_loop(0, PART // H, functools.partial(correct_second, first_pressure), 0)
+    finish.first()
 
     arrived((2,))
     low_w[pl.ds(H + 1 + FIRST, REST), :] = up_recv[2][pl.ds(REST, REST), :]
-    lax.fori_loop(FIRST // H, ROWS // H, functools.partial(correct_first, last_part), 0)
-    pl.when(last_r)(clear_after)
-    second_flows(PART + 1, 8, 2)
-    second_pressures(PART, 8, (N - PART) // 8)
-    lax.fori_loop(PART // H, N // H, functools.partial(correct_second, last_pressure), 0)
-
-    def correct_radial(j, carry):
-        rows = halo[0, pl.ds(H * j + SHIFT - BASE, H), :]
-        add_row(u2, H * j + 2, 0, -s_low * rows)
-        return carry
-
-    lax.fori_loop(0, N // H, correct_radial, 0)
-
     for some, far, copies in ((no_above, far_up, ups), (no_below, far_down, downs)):
 
         @pl.when(some)
@@ -653,23 +688,34 @@
             copy.wait_send()
 
 
-def store(p2, w2, u2, v2, press_out, vert_out, radial_out, lateral_out, sems):
-    inner = pl.ds(2 * H, N * H)
-    copies = [
-        pltpu.make_async_copy(src, dst, sems.at[i])
-        for i, (src, dst) in enumerate(
-            (
-                (p2, press_out),
-                (w2.at[inner], vert_out),
-                (u2.at[inner], radial_out),
-                (v2.at[inner], lateral_out),
-            )
-        )
-    ]
-    for copy in copies:
-        copy.start()
-    for copy in copies:
-        copy.wait()
+def store(ranges, refs):
+    p2, w2, u2, v2, p0, w0, p1, w1, u1, v1, up_last, down_last, *rest = refs
+    low_w, halo, coef, low_more, high_more, press, vert, radial, lateral, sems = rest
+    finish = finishing(
+        ranges, p0, w0, p1, w1, u1, v1, p2, w2, u2, v2,
+        (None, None, up_last), (None, None, down_last), low_w, halo, coef, low_more, high_more,
+    )
+
+    def copy(i, src, early, dst, start, count):
+        from_rows, to_rows = pl.ds((start + early) * H, count * H), pl.ds(start * H, count * H)
+        return pltpu.make_async_copy(src.at[from_rows], dst.at[to_rows], sems.at[i])
+
+    done = PART - H
+    finish.radial(0, done)
+    fields = (v2, 2, lateral), (w2, 2, vert), (p2, 0, press)
+    copies = [copy(i, *field, 0, PART) for i, field in enumerate(fields)]
+    copies.append(copy(6, u2, 2, radial, 0, done))
+    for one in copies:
+        one.start()
+    finish.last()
+    others = [copy(3 + i, *field, PART, N - PART) for i, field in enumerate(fields)]
+    for one in others:
+        one.start()
+    finish.radial(done, N)
+    others.append(copy(7, u2, 2, radial, done, N - done))
+    others[-1].start()
+    for one in copies + others:
+        one.wait()
 
 
 def solution(mesh):
@@ -691,28 +737,32 @@
             pltpu.with_memory_space_constraint(x, pltpu.HBM)
             for x in (*flat, stiff, buoy, wind.reshape(1, 128))
         ]
-        result = [field(N), field(N + 4), field(N + 4), field(N + 4)]
+        result = [field(N), field(N + 4), field(N + 4), field(N + 4)] + [field(64)] * 6
+        result += [
+            messages(UP, 3)[2],
+            messages(DOWN, 3)[2],
+            pltpu.VMEM((ROWS + 2 * H, 128), jnp.float32),
+            pltpu.VMEM((3, ROWS, 128), jnp.float32),
+            pltpu.VMEM((17, H, 128), jnp.float32),
+            field(1),
+            field(1),
+        ]
         state = pl.pallas_call(
             lambda *refs: both_steps(ranges, heights, *refs),
             out_shape=result,
             in_specs=[pl.BlockSpec(memory_space=pltpu.HBM)] * 7,
-            out_specs=[pl.BlockSpec(memory_space=pltpu.VMEM)] * 4,
-            scratch_shapes=[field(64)] * 8
+            out_specs=[pl.BlockSpec(memory_space=pltpu.VMEM)] * len(result),
+            scratch_shapes=[field(64)] * 2
             + [
                 field(1),
                 field(1),
                 pltpu.VMEM((1, 128), jnp.float32),
                 messages(UP, 3),
-                messages(UP, 3),
+                messages(UP, 3)[:2],
                 messages(DOWN, 3),
-                messages(DOWN, 3),
+                messages(DOWN, 3)[:2],
                 messages(UP, 3)[1],
                 messages(DOWN, 3)[1],
-                pltpu.VMEM((ROWS + 2 * H, 128), jnp.float32),
-                pltpu.VMEM((3, ROWS, 128), jnp.float32),
-                pltpu.VMEM((16, H, 128), jnp.float32),
-                field(1),
-                field(1),
                 pltpu.SemaphoreType.DMA((7,)),
                 pltpu.SemaphoreType.DMA((12,)),
                 pltpu.SemaphoreType.DMA((11,)),
@@ -724,11 +774,11 @@
             ),
         )(*arguments)
         out = pl.pallas_call(
-            store,
+            lambda *refs: store(ranges, refs),
             out_shape=[jax.ShapeDtypeStruct((N * H, 128), jnp.float32)] * 4,
-            in_specs=[pl.BlockSpec(memory_space=pltpu.VMEM)] * 4,
+            in_specs=[pl.BlockSpec(memory_space=pltpu.VMEM)] * len(result),
             out_specs=[pl.BlockSpec(memory_space=pltpu.HBM)] * 4,
-            scratch_shapes=[pltpu.SemaphoreType.DMA((4,))],
+            scratch_shapes=[pltpu.SemaphoreType.DMA((8,))],
             compiler_params=pltpu.CompilerParams(vmem_limit_bytes=24 * 2**20),
         )(*state)
         return tuple(x.reshape(N, H, 128) for x in out)

time: 36 us -> 35.9 us (level)
    pallas_call x1, Pallas kernels: 34.3 us -> 33.8 us  [on_device(): pl.pallas_call(lambda *refs: both_steps(ranges, heights, *refs), out_shap...]
    pallas_call x1, Pallas kernels: 0.91 us -> 1.32 us  [on_device(): pl.pallas_call(lambda *refs: store(ranges, refs), out_shape=[jax.ShapeDty...]
where the time goes in v6:
time: 35.9 us; the launch traced here: 35.8 us
  Pallas kernels  35.1 us (98%)
  between operations  0.64 us (2%)
    pallas_call x1, Pallas kernels, on_device(): pl.pallas_call(lambda *refs: both_steps(ranges, heights, *refs), out_shap...  33.8 us
    pallas_call x1, Pallas kernels, on_device(): pl.pallas_call(lambda *refs: store(ranges, refs), out_shape=[jax.ShapeDty...  1.32 us

profile of v6, /device:TPU:463, one launch (start us, length us, event | category | flops | bytes accessed | tf_op | source)
XLA Modules:
  0.0 35.8 jit_solution(7551208180614985929)
XLA Ops:
  0.6 33.8 %shard_map.102 = (f32[384,128]{1,0:T(8,128)S(1)}, f32[416,128]{1,0:T(8,128)S(1)}, f32[416,128]{1,0:T(8,128)S(1)}, f32[416,128]{1,0:T(8,128)S(1)}, f32[512,128]{1...) custom-call(f32[384,128]{1,0:T(8,128)} %bitcast.9, ...), custom_call_target="tpu_custom_call" | custom-call | tf_op jit(solution)/shard_map/pallas_call | solution.py:750
  34.4 1.3 %shard_map.103 = (f32[384,128]{1,0:T(8,128)}, f32[384,128]{1,0:T(8,128)}, f32[384,128]{1,0:T(8,128)}, f32[384,128]{1,0:T(8,128)}) custom-call(f32[384,128]{1,0:T(8,128)S(1)} %get-tuple-element.25.refs_0_, f32[416,128]{1,0:T(8,128)S(1)} %get-tuple-element.26.refs_1_, f32[416,128]{1,0:T(8,128)S(1)} %get-tuple-element.27.refs_2_, ...), custom_call_target="tpu_custom_call" | custom-call | tf_op jit(solution)/shard_map/pallas_call | solution.py:776
